TPU v7x, 128 devices: a whole 4x4x4 slice. The times are simulated.
128 devices in a mesh: fsdp: 32 (over x, z, core), sub: 4 (over y).
Axes of the slice: x: 4, y: 4, z: 4, core: 2. Of those that a mesh axis runs over, the one named last changes fastest.
Arguments:
- tokens: bfloat16 [16384, 1536], P(('fsdp', 'sub')), may hold values from -6 to 6
- cotangent: float32 [16384, 1536], P(('fsdp', 'sub')), may hold values from -6 to 6
- seq_lengths: int32 [256], replicated, may hold values from 1 to 127, as said below
- seq_owner: int32 [256], replicated, may hold values from 0 to 127, as said below
- inner_weight: float32 [2, 1536, 6144], P(None, ('fsdp', 'sub')), may hold values from -0.15625 to 0.15625
- inner_moment: float32 [2, 1536, 6144], P(None, ('fsdp', 'sub')), may hold values from -24 to 24
- inner_square: float32 [2, 1536, 6144], P(None, ('fsdp', 'sub')), may hold values from 1.4760361 to 5.9041443
- state_weight: float32 [2, 1536, 256], P(None, ('fsdp', 'sub')), may hold values from -0.15625 to 0.15625
- state_moment: float32 [2, 1536, 256], P(None, ('fsdp', 'sub')), may hold values from -24 to 24
- state_square: float32 [2, 1536, 256], P(None, ('fsdp', 'sub')), may hold values from 1.4760361 to 5.9041443
- step_weight: float32 [2, 1536, 48], P(None, ('fsdp', 'sub')), may hold values from -0.15625 to 0.15625
- step_moment: float32 [2, 1536, 48], P(None, ('fsdp', 'sub')), may hold values from -24 to 24
- step_square: float32 [2, 1536, 48], P(None, ('fsdp', 'sub')), may hold values from 1.4760361 to 5.9041443
- out_weight: float32 [2, 3072, 1536], P(None, ('fsdp', 'sub')), may hold values from -0.109375 to 0.109375
- out_moment: float32 [2, 3072, 1536], P(None, ('fsdp', 'sub')), may hold values from -40 to 40
- out_square: float32 [2, 3072, 1536], P(None, ('fsdp', 'sub')), may hold values from 4.1001 to 16.4004
- conv_weight: float32 [2, 3328, 5], P(None, ('fsdp', 'sub')), may hold values from -3 to 3
- conv_moment: float32 [2, 3328, 5], P(None, ('fsdp', 'sub')), may hold values from -40 to 40
- conv_square: float32 [2, 3328, 5], P(None, ('fsdp', 'sub')), may hold values from 4.1001 to 16.4004
- gains: float32 [2, 4608], P(None, ('fsdp', 'sub')), may hold values from 0.5 to 1.5
- gain_moment: float32 [2, 4608], P(None, ('fsdp', 'sub')), may hold values from -40 to 40
- gain_square: float32 [2, 4608], P(None, ('fsdp', 'sub')), may hold values from 4.1001 to 16.4004
- head_params: float32 [2, 3, 48], P(None, None, 'sub')
- head_moment: float32 [2, 3, 48], P(None, None, 'sub'), may hold values from -192 to 192
- head_square: float32 [2, 3, 48], P(None, None, 'sub'), may hold values from 94.46631 to 377.86523
Outputs:
- activations: float32 [16384, 1536], P(('fsdp', 'sub'))
- input_grad: float32 [16384, 1536], P(('fsdp', 'sub'))
- new_inner_weight: float32 [2, 1536, 6144], P(None, ('fsdp', 'sub'))
- new_inner_moment: float32 [2, 1536, 6144], P(None, ('fsdp', 'sub'))
- new_inner_square: float32 [2, 1536, 6144], P(None, ('fsdp', 'sub'))
- new_state_weight: float32 [2, 1536, 256], P(None, ('fsdp', 'sub'))
- new_state_moment: float32 [2, 1536, 256], P(None, ('fsdp', 'sub'))
- new_state_square: float32 [2, 1536, 256], P(None, ('fsdp', 'sub'))
- new_step_weight: float32 [2, 1536, 48], P(None, ('fsdp', 'sub'))
- new_step_moment: float32 [2, 1536, 48], P(None, ('fsdp', 'sub'))
- new_step_square: float32 [2, 1536, 48], P(None, ('fsdp', 'sub'))
- new_out_weight: float32 [2, 3072, 1536], P(None, ('fsdp', 'sub'))
- new_out_moment: float32 [2, 3072, 1536], P(None, ('fsdp', 'sub'))
- new_out_square: float32 [2, 3072, 1536], P(None, ('fsdp', 'sub'))
- new_conv_weight: float32 [2, 3328, 5], P(None, ('fsdp', 'sub'))
- new_conv_moment: float32 [2, 3328, 5], P(None, ('fsdp', 'sub'))
- new_conv_square: float32 [2, 3328, 5], P(None, ('fsdp', 'sub'))
- new_gains: float32 [2, 4608], P(None, ('fsdp', 'sub'))
- new_gain_moment: float32 [2, 4608], P(None, ('fsdp', 'sub'))
- new_gain_square: float32 [2, 4608], P(None, ('fsdp', 'sub'))
- new_head_params: float32 [2, 3, 48], P(None, None, 'sub')
- new_head_moment: float32 [2, 3, 48], P(None, None, 'sub')
- new_head_square: float32 [2, 3, 48], P(None, None, 'sub')
- grad_inner: float32 [2, 1536, 6144], P(None, ('fsdp', 'sub'))
- grad_state: float32 [2, 1536, 256], P(None, ('fsdp', 'sub'))
- grad_step: float32 [2, 1536, 48], P(None, ('fsdp', 'sub'))
- grad_out: float32 [2, 3072, 1536], P(None, ('fsdp', 'sub'))
- grad_conv: float32 [2, 3328, 5], P(None, ('fsdp', 'sub'))
- grad_gains: float32 [2, 4608], P(None, ('fsdp', 'sub'))
- grad_head: float32 [2, 3, 48], P(None, None, 'sub')
Inputs may be any that keep to these rules, and one draw needn't show every extreme that they name: `seq_lengths`: each device owns exactly two sequences; the two sequences of one device hold 64 to 128 tokens together, exactly 128 on some device in every draw, and lengths 1 and 127 occur in every draw. `seq_owner`: every device index appears exactly twice.
All inputs are finite; a program needn't handle non-finite values.
Results may differ from a plain program's by a relative error of at most 0.02.
The roundings to bfloat16 on the way count: a program that leaves them out, or rounds other values in their place, can miss the bound.
Values may be sent and summed in bfloat16 or wider, within the bound.
A program may use at most 512 MiB of HBM per device.

v0:
```python
from functools import partial

import jax
import jax.numpy as jnp
from jax import lax
from jax.sharding import PartitionSpec as P

STEP = 10


EPS_NORM = 1e-05
BETA_ONE = 0.9
BETA_TWO = 0.999
ADAM_EPS = 1e-08
RATE_MATRIX = 0.05
RATE_VECTOR = 0.5
RATE_HEADS = 2.0
WEIGHT_DECAY = 0.1


def seq_layout(seq_lengths, seq_owner, device, slots):
    owned = (seq_owner == device).astype(jnp.int32)
    before = jnp.cumsum(owned) - owned
    length_one = jnp.sum(seq_lengths * owned * (before == 0).astype(jnp.int32))
    length_two = jnp.sum(seq_lengths * owned * (before == 1).astype(jnp.int32))
    place = jnp.arange(slots, dtype=jnp.int32)
    segment = jnp.where(
        place < length_one, 0, jnp.where(place < length_one + length_two, 1, 2)
    ).astype(jnp.int32)
    live = (place < length_one + length_two).astype(jnp.float32)
    return (segment, live)


def rms_scale(values, gain):
    return values * lax.rsqrt(jnp.mean(values * values, axis=1, keepdims=True) + EPS_NORM) * gain


def prepare(proj_zx, proj_bc, proj_dt, conv_par, head_layer, segment):
    slots = proj_zx.shape[0]
    inner_width = proj_zx.shape[1] // 2
    state = proj_bc.shape[1] // 2
    nheads = head_layer.shape[1]
    head_size = inner_width // nheads
    taps = conv_par.shape[1] - 1
    conv_in = jnp.concatenate([proj_zx[:, inner_width:], proj_bc], axis=1)
    conved = conv_par[:, taps] + jnp.zeros_like(conv_in)
    for lag in range(taps):
        moved = jnp.pad(conv_in, ((lag, 0), (0, 0)))[:slots]
        earlier = jnp.pad(segment, (lag, 0), constant_values=-1)[:slots]
        same = (earlier == segment).astype(jnp.float32)[:, None]
        conved = conved + conv_par[:, taps - 1 - lag] * moved * same
    active = jax.nn.silu(conved)
    values = active[:, :inner_width]
    state_in = active[:, inner_width : inner_width + state]
    state_out = active[:, inner_width + state :]
    step_size = jax.nn.softplus(proj_dt + head_layer[0])
    level = jnp.cumsum(step_size * -jnp.exp(head_layer[1]), axis=0)
    place = jnp.arange(slots)
    allowed = ((place[:, None] >= place[None, :]) & (segment[:, None] == segment[None, :]))[None]
    gap = level.T[:, :, None] - level.T[:, None, :]
    decay = jnp.where(allowed, jnp.exp(jnp.where(allowed, gap, 0.0)), 0.0)
    scaled = values.reshape(slots, nheads, head_size) * step_size[:, :, None]
    skip_term = values * jnp.repeat(head_layer[2], head_size)
    z_gate = jax.nn.silu(proj_zx[:, :inner_width])
    return (state_in, state_out, scaled, decay, skip_term, z_gate)


def finish(ssd_out, skip_term, z_gate, gate_gain):
    return rms_scale((ssd_out + skip_term) * z_gate, gate_gain)


def fetch(masters, layer):
    mat_zx, mat_bc, mat_dt, mat_out, conv_taps, norm_gains = [
        master[layer].astype(jnp.bfloat16) for master in masters
    ]
    return (
        lax.all_gather(mat_zx, ("fsdp", "sub"), axis=0, tiled=True),
        lax.all_gather(mat_bc, ("fsdp", "sub"), axis=0, tiled=True),
        lax.all_gather(mat_dt, ("fsdp", "sub"), axis=0, tiled=True),
        lax.all_gather(mat_out, ("fsdp", "sub"), axis=0, tiled=True),
        lax.all_gather(conv_taps, ("fsdp", "sub"), axis=0, tiled=True),
        lax.all_gather(norm_gains, ("fsdp", "sub"), axis=0, tiled=True),
    )


def fetch_again(masters, layer):
    mat_zx, mat_bc, mat_dt, mat_out, conv_taps, norm_gains = [
        master[layer].astype(jnp.bfloat16) for master in masters
    ]
    return (
        lax.all_gather(mat_zx, ("fsdp", "sub"), axis=0, tiled=True),
        lax.all_gather(mat_bc, ("fsdp", "sub"), axis=0, tiled=True),
        lax.all_gather(mat_dt, ("fsdp", "sub"), axis=0, tiled=True),
        lax.all_gather(mat_out, ("fsdp", "sub"), axis=0, tiled=True),
        lax.all_gather(conv_taps, ("fsdp", "sub"), axis=0, tiled=True),
        lax.all_gather(norm_gains, ("fsdp", "sub"), axis=0, tiled=True),
    )


def reduce_grads(grads):
    devices = lax.axis_size(("fsdp", "sub"))
    flat_rows = [grad.reshape(devices, -1) for grad in grads]
    widths = [flat.shape[1] for flat in flat_rows]
    joined = jnp.concatenate(flat_rows, axis=1)
    length_all = joined.shape[1]
    padded = -(-length_all // 1024) * 1024
    joined = jnp.pad(joined, ((0, 0), (0, padded - length_all))).reshape(devices * 8, padded // 8)
    owned_part = lax.psum_scatter(joined, ("fsdp", "sub"), scatter_dimension=0, tiled=True).reshape(
        -1
    )
    pieces = []
    offset = 0
    for number in range(len(grads)):
        shard_shape = (grads[number].shape[0] // devices,) + grads[number].shape[1:]
        pieces.append(owned_part[offset : offset + widths[number]].reshape(shard_shape))
        offset = offset + widths[number]
    return tuple(pieces)


def layer_forward(resid, segment, live, weights, head_layer):
    mat_zx, mat_bc, mat_dt, mat_out, conv_taps, norm_gains = weights
    width = resid.shape[1]
    slots = resid.shape[0]
    gain_full = norm_gains.astype(jnp.float32)
    norm_value, norm_pull = jax.vjp(rms_scale, resid, gain_full[:width])
    normed = norm_value.astype(jnp.bfloat16) * live[:, None].astype(jnp.bfloat16)
    proj_zx = jnp.dot(normed, mat_zx, preferred_element_type=jnp.float32)
    proj_bc = jnp.dot(normed, mat_bc, preferred_element_type=jnp.float32)
    proj_dt = jnp.dot(normed, mat_dt, preferred_element_type=jnp.float32)
    prep_value, prep_pull = jax.vjp(
        partial(prepare, segment=segment),
        proj_zx,
        proj_bc,
        proj_dt,
        conv_taps.astype(jnp.float32),
        head_layer,
    )
    state_in, state_out, scaled, decay, skip_term, z_gate = prep_value
    state_in_low = state_in.astype(jnp.bfloat16)
    state_out_low = state_out.astype(jnp.bfloat16)
    inner = jnp.einsum("tn,sn->ts", state_out_low, state_in_low, preferred_element_type=jnp.float32)
    mix_low = (inner[None] * decay).astype(jnp.bfloat16)
    scaled_low = scaled.astype(jnp.bfloat16)
    ssd_out = jnp.einsum(
        "hts,shp->thp", mix_low, scaled_low, preferred_element_type=jnp.float32
    ).reshape(slots, -1)
    gate_value, gate_pull = jax.vjp(finish, ssd_out, skip_term, z_gate, gain_full[width:])
    gate_low = gate_value.astype(jnp.bfloat16)
    branch = jnp.dot(gate_low, mat_out, preferred_element_type=jnp.float32)
    saved = (
        normed,
        norm_pull,
        prep_pull,
        gate_pull,
        state_in_low,
        state_out_low,
        inner,
        decay,
        mix_low,
        scaled_low,
        gate_low,
    )
    return (resid + live[:, None] * branch, saved)


def layer_backward(upstream, live, weights, saved):
    mat_zx, mat_bc, mat_dt, mat_out, conv_taps, norm_gains = weights
    (
        normed,
        norm_pull,
        prep_pull,
        gate_pull,
        state_in_low,
        state_out_low,
        inner,
        decay,
        mix_low,
        scaled_low,
        gate_low,
    ) = saved
    d_branch = (upstream * live[:, None]).astype(jnp.bfloat16)
    d_gate = jnp.einsum("tk,jk->tj", d_branch, mat_out, preferred_element_type=jnp.float32)
    grad_mat_out = jnp.einsum("tj,tk->jk", gate_low, d_branch, preferred_element_type=jnp.float32)
    d_ssd, d_skip, d_zgate, d_gate_gain = gate_pull(d_gate)
    d_ssd_low = d_ssd.reshape(scaled_low.shape).astype(jnp.bfloat16)
    d_mix = jnp.einsum("thp,shp->hts", d_ssd_low, scaled_low, preferred_element_type=jnp.float32)
    d_scaled = jnp.einsum("hts,thp->shp", mix_low, d_ssd_low, preferred_element_type=jnp.float32)
    d_inner = jnp.sum(d_mix * decay, axis=0).astype(jnp.bfloat16)
    d_decay = d_mix * inner[None]
    d_state_out = jnp.dot(d_inner, state_in_low, preferred_element_type=jnp.float32)
    d_state_in = jnp.einsum("ts,tn->sn", d_inner, state_out_low, preferred_element_type=jnp.float32)
    d_zx, d_bc, d_dt, grad_taps, grad_heads = prep_pull(
        (d_state_in, d_state_out, d_scaled, d_decay, d_skip, d_zgate)
    )
    d_zx = d_zx.astype(jnp.bfloat16)
    d_bc = d_bc.astype(jnp.bfloat16)
    d_dt = d_dt.astype(jnp.bfloat16)
    grad_zx = jnp.einsum("td,tk->dk", normed, d_zx, preferred_element_type=jnp.float32)
    grad_bc = jnp.einsum("td,tk->dk", normed, d_bc, preferred_element_type=jnp.float32)
    grad_dt = jnp.einsum("td,tk->dk", normed, d_dt, preferred_element_type=jnp.float32)
    d_normed = jnp.einsum("tk,dk->td", d_zx, mat_zx, preferred_element_type=jnp.float32)
    d_normed = d_normed + jnp.einsum("tk,dk->td", d_bc, mat_bc, preferred_element_type=jnp.float32)
    d_normed = d_normed + jnp.einsum("tk,dk->td", d_dt, mat_dt, preferred_element_type=jnp.float32)
    d_resid, d_norm_gain = norm_pull(d_normed * live[:, None])
    grads = (
        grad_zx,
        grad_bc,
        grad_dt,
        grad_mat_out,
        grad_taps,
        jnp.concatenate([d_norm_gain, d_gate_gain]),
    )
    return (upstream + d_resid, grads, grad_heads)


def adam(weight, moment, square, grad, rate, decay):
    moment = BETA_ONE * moment + (1.0 - BETA_ONE) * grad
    square = BETA_TWO * square + (1.0 - BETA_TWO) * grad * grad
    corr_one = 1.0 - BETA_ONE**STEP
    corr_two = 1.0 - BETA_TWO**STEP
    weight = weight - rate * (
        moment / corr_one / (jnp.sqrt(square / corr_two) + ADAM_EPS) + decay * weight
    )
    return (weight, moment, square)


def shards(
    tokens,
    cotangent,
    seq_lengths,
    seq_owner,
    inner_weight,
    inner_moment,
    inner_square,
    state_weight,
    state_moment,
    state_square,
    step_weight,
    step_moment,
    step_square,
    out_weight,
    out_moment,
    out_square,
    conv_weight,
    conv_moment,
    conv_square,
    gains,
    gain_moment,
    gain_square,
    head_params,
    head_moment,
    head_square,
):
    device = lax.axis_index(("fsdp", "sub"))
    slots = tokens.shape[0]
    segment, live = seq_layout(seq_lengths, seq_owner, device, slots)
    masters = (inner_weight, state_weight, step_weight, out_weight, conv_weight, gains)
    layers = inner_weight.shape[0]
    all_heads = lax.all_gather(head_params, "sub", axis=2, tiled=True)
    resid = tokens.astype(jnp.float32)
    kept = []
    for layer in range(layers):
        weights = fetch(masters, layer)
        resid, saved = layer_forward(resid, segment, live, weights, all_heads[layer])
        kept.append((weights, saved))
    upstream = cotangent
    reduced = [None] * layers
    head_terms = [None] * layers
    for layer in reversed(range(layers)):
        weights, saved = kept[layer]
        weights = fetch_again(masters, layer)
        upstream, grads, grad_heads = layer_backward(upstream, live, weights, saved)
        reduced[layer] = reduce_grads(grads)
        head_terms[layer] = grad_heads
    head_total = lax.psum(jnp.stack(head_terms), ("fsdp", "sub"))
    per_shard = head_params.shape[2]
    head_grad = lax.dynamic_slice_in_dim(
        head_total, lax.axis_index("sub") * per_shard, per_shard, 2
    )
    states = (
        (inner_weight, inner_moment, inner_square, RATE_MATRIX, WEIGHT_DECAY),
        (state_weight, state_moment, state_square, RATE_MATRIX, WEIGHT_DECAY),
        (step_weight, step_moment, step_square, RATE_MATRIX, WEIGHT_DECAY),
        (out_weight, out_moment, out_square, RATE_MATRIX, WEIGHT_DECAY),
        (conv_weight, conv_moment, conv_square, RATE_VECTOR, 0.0),
        (gains, gain_moment, gain_square, RATE_VECTOR, 0.0),
    )
    results = [resid, upstream]
    summed = []
    for number in range(6):
        weight, moment, square, rate, decay = states[number]
        grad = jnp.stack([item[number] for item in reduced])
        summed.append(grad)
        results.extend(adam(weight, moment, square, grad, rate, decay))
    results.extend(adam(head_params, head_moment, head_square, head_grad, RATE_HEADS, 0.0))
    results.extend(summed)
    results.append(head_grad)
    return tuple(results)


def solution(mesh):
    placed = (
        P(("fsdp", "sub"), None),
        P(("fsdp", "sub"), None),
        P(),
        P(),
        P(None, ("fsdp", "sub"), None),
        P(None, ("fsdp", "sub"), None),
        P(None, ("fsdp", "sub"), None),
        P(None, ("fsdp", "sub"), None),
        P(None, ("fsdp", "sub"), None),
        P(None, ("fsdp", "sub"), None),
        P(None, ("fsdp", "sub"), None),
        P(None, ("fsdp", "sub"), None),
        P(None, ("fsdp", "sub"), None),
        P(None, ("fsdp", "sub"), None),
        P(None, ("fsdp", "sub"), None),
        P(None, ("fsdp", "sub"), None),
        P(None, ("fsdp", "sub"), None),
        P(None, ("fsdp", "sub"), None),
        P(None, ("fsdp", "sub"), None),
        P(None, ("fsdp", "sub")),
        P(None, ("fsdp", "sub")),
        P(None, ("fsdp", "sub")),
        P(None, None, "sub"),
        P(None, None, "sub"),
        P(None, None, "sub"),
    )
    return jax.shard_map(
        shards,
        mesh=mesh,
        in_specs=placed,
        out_specs=(
            P(("fsdp", "sub"), None),
            P(("fsdp", "sub"), None),
            P(None, ("fsdp", "sub"), None),
            P(None, ("fsdp", "sub"), None),
            P(None, ("fsdp", "sub"), None),
            P(None, ("fsdp", "sub"), None),
            P(None, ("fsdp", "sub"), None),
            P(None, ("fsdp", "sub"), None),
            P(None, ("fsdp", "sub"), None),
            P(None, ("fsdp", "sub"), None),
            P(None, ("fsdp", "sub"), None),
            P(None, ("fsdp", "sub"), None),
            P(None, ("fsdp", "sub"), None),
            P(None, ("fsdp", "sub"), None),
            P(None, ("fsdp", "sub"), None),
            P(None, ("fsdp", "sub"), None),
            P(None, ("fsdp", "sub"), None),
            P(None, ("fsdp", "sub")),
            P(None, ("fsdp", "sub")),
            P(None, ("fsdp", "sub")),
            P(None, None, "sub"),
            P(None, None, "sub"),
            P(None, None, "sub"),
            P(None, ("fsdp", "sub"), None),
            P(None, ("fsdp", "sub"), None),
            P(None, ("fsdp", "sub"), None),
            P(None, ("fsdp", "sub"), None),
            P(None, ("fsdp", "sub"), None),
            P(None, ("fsdp", "sub")),
            P(None, None, "sub"),
        ),
        check_vma=False,
    )
```

profile of v0, /device:TPU:0, one launch (start us, length us, event | category | flops | bytes accessed | tf_op | source)
XLA Modules:
  0.0 2478.6 jit_solution(4139546319555600579)
XLA Ops:
  12.6 69.0 %all-reduce.45 = (bf16[4608]{0:T(1024)(128)(2,1)S(1)}, bf16[4608]{0:T(1024)(128)(2,1)S(1)}) all-reduce(bf16[4608]{0:T(1024)(128)(2,1)S(1)} %dynamic-update-slice, bf16[4608]{0:T(1024)(128)(2,1)S(1)} %dynamic-update-slice.1), channel_id=3, replica_groups=mesh['fsdp'=32,'sub'=4] {'fsdp','sub'}, use_global_device_ids=true, to_apply=%add.43 | all-reduce | flops 9216 | bytes 36864
  82.2 59.0 %all-gather.4 = bf16[1,1536,48]{2,0,1:T(2,128)(2,1)S(1)} all-gather(bf16[1,12,48]{2,0,1:T(2,128)(2,1)S(1)} %get-tuple-element.314), channel_id=6, replica_groups=mesh['fsdp'=32,'sub'=4] {'fsdp','sub'}, dimensions={1}, use_global_device_ids=true | all-gather | bytes 148608 | tf_op jit(solution)/shard_map/all_gather | solution.py:79
  144.5 11.9 all_gather.52
  160.3 66.7 %all-gather = bf16[1,3328,5]{2,0,1:T(2,128)(2,1)S(1)} all-gather(bf16[1,26,5]{2,0,1:T(2,128)(2,1)S(1)} %get-tuple-element.310), channel_id=2, replica_groups=mesh['fsdp'=32,'sub'=4] {'fsdp','sub'}, dimensions={1}, use_global_device_ids=true | all-gather | bytes 33540 | tf_op jit(solution)/shard_map/all_gather | solution.py:81
  229.5 60.6 %all-gather.10 = bf16[1,1536,48]{2,0,1:T(2,128)(2,1)S(1)} all-gather(bf16[1,12,48]{2,0,1:T(2,128)(2,1)S(1)} %get-tuple-element.313), channel_id=12, replica_groups=mesh['fsdp'=32,'sub'=4] {'fsdp','sub'}, dimensions={1}, use_global_device_ids=true | all-gather | bytes 148608 | tf_op jit(solution)/shard_map/all_gather | solution.py:79
  291.7 67.7 %all-gather.6 = bf16[1,3328,5]{2,0,1:T(2,128)(2,1)S(1)} all-gather(bf16[1,26,5]{2,0,1:T(2,128)(2,1)S(1)} %get-tuple-element.309), channel_id=8, replica_groups=mesh['fsdp'=32,'sub'=4] {'fsdp','sub'}, dimensions={1}, use_global_device_ids=true | all-gather | bytes 33540 | tf_op jit(solution)/shard_map/all_gather | solution.py:81
  366.1 65.4 %all-gather.3 = bf16[1,1536,256]{2,0,1:T(2,128)(2,1)S(1)} all-gather(bf16[1,12,256]{2,0,1:T(2,128)(2,1)S(1)} %get-tuple-element.312), channel_id=5, replica_groups=mesh['fsdp'=32,'sub'=4] {'fsdp','sub'}, dimensions={1}, use_global_device_ids=true | all-gather | bytes 792576 | tf_op jit(solution)/shard_map/all_gather | solution.py:78
  433.7 71.2 %all-gather.9 = bf16[1,1536,256]{2,0,1:T(2,128)(2,1)} all-gather(bf16[1,12,256]{2,0,1:T(2,128)(2,1)S(1)} %get-tuple-element.311), channel_id=11, replica_groups=mesh['fsdp'=32,'sub'=4] {'fsdp','sub'}, dimensions={1}, use_global_device_ids=true | all-gather | bytes 792576 | tf_op jit(solution)/shard_map/all_gather | solution.py:78
  504.9 22.9 fusion.6
  550.6 25.4 %fusion.2 = f32[128,6144]{1,0:T(8,128)} fusion(bf16[128,1536]{1,0:T(8,128)(2,1)S(1)} %fusion.83, bf16[1,1536,6144]{2,0,1:T(2,128)(2,1)} %all-gather.21.cloned.1.call-done), kind=kOutput, calls=%fused_computation.2 | convolution fusion | flops 2415919104 | bytes 22413312 | tf_op jit(solution)/shard_map/dot_general | solution.py:127
  632.6 25.8 %fusion = f32[128,1536]{1,0:T(8,128)S(1)} fusion(bf16[1,1536,6144]{2,0,1:T(2,128)(2,1)} %all-gather.21.cloned.1.call-done, f32[128,3072]{1,0:T(8,128)S(1)} %split.18, f32[128,3072]{1,0:T(8,128)S(1)} %copy-done.39), kind=kOutput, calls=%fused_computation | convolution fusion | flops 2417491968 | bytes 22806528 | tf_op jit(solution)/shard_map/tk,dk->td/dot_general | solution.py:201
  698.0 14.7 fusion.92
  716.5 8.1 fusion.159
  728.0 37.2 %reshape.493 = f32[128,73728]{1,0:T(8,128)} reshape(f32[1536,6144]{1,0:T(8,128)} %fusion.92) | data formatting | bytes 75497472 | tf_op jit(solution)/shard_map/reshape | solution.py:102
  765.2 27.2 %constant_dynamic-update-slice_fusion.3 = f32[128,114406]{1,0:T(8,128)} fusion(f32[128,73728]{1,0:T(8,128)} %reshape.493), kind=kLoop, calls=%fused_computation.249 | loop fusion | bytes 75497472
  795.1 19.6 reshape.496
  814.7 9.4 multiply_reduce_fusion.5
  832.2 55.5 %dynamic-update-slice.9 = f32[128,114406]{1,0:T(8,128)} dynamic-update-slice(f32[128,114406]{1,0:T(8,128)} %dynamic-update-slice.8, f32[128,36864]{1,0:T(8,128)} %reshape.496, s32[]{} %constant.304, s32[]{} %constant.310) | dynamic-update-slice | bytes 37748740
  891.1 39.0 %pad.208 = f32[128,114688]{1,0:T(8,128)} pad(f32[128,114406]{1,0:T(8,128)} %dynamic-update-slice.11, f32[]{:T(128)} %constant.61.clone.1), padding=0_0x0_282 | pad | bytes 117296128 | tf_op jit(solution)/shard_map/jit(_pad)/pad | solution.py:107
  930.1 43.2 %reshape.499 = f32[1024,14336]{1,0:T(8,128)} reshape(f32[128,114688]{1,0:T(8,128)} %pad.208) | data formatting | bytes 117440512 | tf_op jit(solution)/shard_map/reshape | solution.py:107
  983.6 15.4 fusion.93
  998.9 37.3 %reshape.485 = f32[128,73728]{1,0:T(8,128)} reshape(f32[1536,6144]{1,0:T(8,128)} %fusion.93) | data formatting | bytes 75497472 | tf_op jit(solution)/shard_map/reshape | solution.py:102
  1042.8 8.9 fusion.160
  1051.7 19.6 reshape.488
  1075.8 25.4 %fusion.4 = f32[128,1536]{1,0:T(8,128)S(1)} fusion(bf16[1,1536,6144]{2,0,1:T(2,128)(2,1)} %all-gather.17.cloned.1.call-done, f32[128,3072]{1,0:T(8,128)S(1)} %copy-done.37, f32[128,3072]{1,0:T(8,128)} %get-tuple-element.288), kind=kOutput, calls=%fused_computation.4 | convolution fusion | flops 2417491968 | bytes 22806528 | tf_op jit(solution)/shard_map/tk,dk->td/dot_general | solution.py:201
  1104.7 27.5 %constant_dynamic-update-slice_fusion.1 = f32[128,114406]{1,0:T(8,128)} fusion(f32[128,73728]{1,0:T(8,128)} %reshape.485), kind=kLoop, calls=%fused_computation.247 | loop fusion | bytes 75497472
  1136.8 55.8 %dynamic-update-slice.15 = f32[128,114406]{1,0:T(8,128)} dynamic-update-slice(f32[128,114406]{1,0:T(8,128)} %dynamic-update-slice.14, f32[128,36864]{1,0:T(8,128)} %reshape.488, s32[]{} %constant.304, s32[]{} %constant.310) | dynamic-update-slice | bytes 37748740
  1195.9 39.3 %pad.202 = f32[128,114688]{1,0:T(8,128)} pad(f32[128,114406]{1,0:T(8,128)} %dynamic-update-slice.17, f32[]{:T(128)} %constant.61.clone.1), padding=0_0x0_282 | pad | bytes 117296128 | tf_op jit(solution)/shard_map/jit(_pad)/pad | solution.py:107
  1235.3 43.6 %reshape.491 = f32[1024,14336]{1,0:T(8,128)} reshape(f32[128,114688]{1,0:T(8,128)} %pad.202) | data formatting | bytes 117440512 | tf_op jit(solution)/shard_map/reshape | solution.py:107
  1287.3 70.8 %psum.7 = f32[2,3,48]{2,1,0:T(4,128)} all-reduce(f32[2,3,48]{2,1,0:T(4,128)} %pad_maximum_fusion.7), channel_id=1, replica_groups=mesh['fsdp'=32,'sub'=4] {'fsdp','sub'}, use_global_device_ids=true, to_apply=%region_48.50 | all-reduce | flops 288 | bytes 2304 | tf_op jit(solution)/shard_map/psum | solution.py:275
  1370.2 344.4 %reduce-scatter.5.cloned.1.call-done = f32[8,14336]{1,0:T(8,128)} async-done(((f32[1024,14336]{1,0:T(8,128)}), f32[8,14336]{1,0:T(8,128)}) %reduce-scatter.5.cloned.1.call-update) | async-done | bytes 458768 | tf_op jit(solution)/shard_map/reduce_scatter | solution.py:108
  1715.9 740.5 %reduce-scatter.3.cloned.1.call-done = f32[8,14336]{1,0:T(8,128)} async-done(((f32[1024,14336]{1,0:T(8,128)}), f32[8,14336]{1,0:T(8,128)}) %reduce-scatter.3.cloned.1.call-update) | async-done | bytes 458768 | tf_op jit(solution)/shard_map/reduce_scatter | solution.py:108
  (610 shorter events, 232.2 us)
Async XLA Ops:
  7.2 74.4 %copy-start.177 = (s32[256]{0:T(256)S(1)}, s32[256]{0:T(256)}, u32[]{:S(2)}) copy-start(s32[256]{0:T(256)} %param.29) | copy-start | bytes 3076
  7.2 74.8 %copy-start.167 = (f32[2,3,12]{2,0,1:T(2,128)S(1)}, f32[2,3,12]{2,0,1:T(2,128)}, u32[]{:S(2)}) copy-start(f32[2,3,12]{2,0,1:T(2,128)} %param.48) | copy-start | bytes 868
  7.2 74.9 %copy-start.121 = (f32[2,12,48]{2,0,1:T(2,128)S(1)}, f32[2,12,48]{2,0,1:T(2,128)}, u32[]{:S(2)}) copy-start(f32[2,12,48]{2,0,1:T(2,128)} %param.36) | copy-start | bytes 13828
  7.3 497.6 %all-gather.17.cloned.1.call-start = ((), (), s32[]{:S(2)}) async-start(), calls=%async_computation.4 | async-start | bytes 38043648 | tf_op jit(solution)/shard_map/all_gather | solution.py:77
  9.9 132.6 %copy-start.178 = (s32[256]{0:T(256)S(1)}, s32[256]{0:T(256)}, u32[]{:S(2)}) copy-start(s32[256]{0:T(256)} %param.28) | copy-start | bytes 3076
  9.9 146.6 %copy-start.10 = (bf16[128,1536]{1,0:T(8,128)(2,1)S(1)}, bf16[128,1536]{1,0:T(8,128)(2,1)}, u32[]{:S(2)}) copy-start(bf16[128,1536]{1,0:T(8,128)(2,1)} %param.26) | copy-start | bytes 1179652
  9.9 532.7 %all-gather.19.cloned.1.call-start = ((), (), s32[]{:S(2)}) async-start(), calls=%async_computation.5 | async-start | bytes 9510912 | tf_op jit(solution)/shard_map/all_gather | solution.py:80
  10.7 539.9 %all-gather.21.cloned.1.call-start = ((), (), s32[]{:S(2)}) async-start(), calls=%async_computation.6 | async-start | bytes 38043648 | tf_op jit(solution)/shard_map/all_gather | solution.py:77
  11.4 583.6 %all-gather.23.cloned.1.call-start = ((), (), s32[]{:S(2)}) async-start(), calls=%async_computation.7 | async-start | bytes 9510912 | tf_op jit(solution)/shard_map/all_gather | solution.py:80
  12.0 1702.7 %reduce-scatter.5.cloned.1.call-start = ((), (), s32[]{:S(2)}) async-start(), calls=%async_computation.3 | async-start | bytes 59179008 | tf_op jit(solution)/shard_map/reduce_scatter | solution.py:108
  156.4 275.1 %copy-start.142 = (bf16[128]{0:T(256)(128)(2,1)}, bf16[128]{0:T(256)(128)(2,1)S(1)}, u32[]{:S(2)}) copy-start(bf16[128]{0:T(256)(128)(2,1)S(1)} %fusion.158) | copy-start | bytes 772
  156.4 275.0 %copy-start.69 = (f32[1536]{0:T(1024)}, f32[1536]{0:T(1024)S(1)}, u32[]{:S(2)}) copy-start(f32[1536]{0:T(1024)S(1)} %slice_reduce_fusion.15) | copy-start | bytes 18436
  158.2 273.3 %copy-start.126 = (f32[128]{0:T(128)}, f32[128]{0:T(128)S(1)}, u32[]{:S(2)}) copy-start(f32[128]{0:T(128)S(1)} %fusion.146) | copy-start | bytes 1540
  361.9 354.6 %copy-start.59 = (f32[1,3072]{1,0:T(1,128)}, f32[1,3072]{1,0:T(1,128)S(1)}, u32[]{:S(2)}) copy-start(f32[1,3072]{1,0:T(1,128)S(1)} %slice.350) | copy-start | bytes 36868
  362.6 353.9 %copy-start.124 = (f32[128]{0:T(128)}, f32[128]{0:T(128)S(1)}, u32[]{:S(2)}) copy-start(f32[128]{0:T(128)S(1)} %compare_convert_fusion.3) | copy-start | bytes 1540
  542.5 137.2 %copy-start.2 = (f32[128,3072]{1,0:T(8,128)}, f32[128,3072]{1,0:T(8,128)S(1)}, u32[]{:S(2)}) copy-start(f32[128,3072]{1,0:T(8,128)S(1)} %get-tuple-element.282) | copy-start | bytes 4718596
  548.5 27.5 %copy-start.12 = (f32[128,1536]{1,0:T(8,128)}, f32[128,1536]{1,0:T(8,128)S(1)}, u32[]{:S(2)}) copy-start(f32[128,1536]{1,0:T(8,128)S(1)} %get-tuple-element.322) | copy-start | bytes 2359300
  548.5 27.5 %copy-start.183 = (f32[128]{0:T(128)}, f32[128]{0:T(128)S(1)}, u32[]{:S(2)}) copy-start(f32[128]{0:T(128)S(1)} %get-tuple-element.321) | copy-start | bytes 1540
  548.5 27.5 %copy-start.171 = (f32[128]{0:T(128)}, f32[128]{0:T(128)S(1)}, u32[]{:S(2)}) copy-start(f32[128]{0:T(128)S(1)} %fusion.148) | copy-start | bytes 1540
  594.0 122.5 %copy-start = (f32[128,3072]{1,0:T(8,128)}, f32[128,3072]{1,0:T(8,128)S(1)}, u32[]{:S(2)}) copy-start(f32[128,3072]{1,0:T(8,128)S(1)} %get-tuple-element.277) | copy-start | bytes 4718596
  630.0 28.4 %copy-start.26 = (f32[128,3328]{1,0:T(8,128)}, f32[128,3328]{1,0:T(8,128)S(1)}, u32[]{:S(2)}) copy-start(f32[128,3328]{1,0:T(8,128)S(1)} %fusion.42) | copy-start | bytes 5111812
  630.2 28.2 %copy-start.34 = (f32[128,3072]{1,0:T(8,128)}, f32[128,3072]{1,0:T(8,128)S(1)}, u32[]{:S(2)}) copy-start(f32[128,3072]{1,0:T(8,128)S(1)} %split.18) | copy-start | bytes 4718596
  765.2 27.2 %copy-start.42 = (f32[1536,256]{1,0:T(8,128)S(1)}, f32[1536,256]{1,0:T(8,128)}, u32[]{:S(2)}) copy-start(f32[1536,256]{1,0:T(8,128)} %fusion.113) | copy-start | bytes 4718596
  973.4 1483.0 %reduce-scatter.3.cloned.1.call-start = ((), (), s32[]{:S(2)}) async-start(), calls=%async_computation.2 | async-start | bytes 59179008 | tf_op jit(solution)/shard_map/reduce_scatter | solution.py:108
  1104.7 27.5 %copy-start.41 = (f32[128,3072]{1,0:T(8,128)S(1)}, f32[128,3072]{1,0:T(8,128)}, u32[]{:S(2)}) copy-start(f32[128,3072]{1,0:T(8,128)} %reshape.486) | copy-start | bytes 4718596
  1136.8 55.8 %copy-start.75 = (f32[128,130]{1,0:T(8,128)S(1)}, f32[128,130]{1,0:T(8,128)}, u32[]{:S(2)}) copy-start(f32[128,130]{1,0:T(8,128)} %reshape.489) | copy-start | bytes 199684
  1278.9 85.2 %copy-start.1 = (f32[128,3072]{1,0:T(8,128)S(1)}, f32[128,3072]{1,0:T(8,128)}, u32[]{:S(2)}) copy-start(f32[128,3072]{1,0:T(8,128)} %copy-done) | copy-start | bytes 4718596
  1279.0 85.2 %copy-start.14 = (f32[128,1536]{1,0:T(8,128)S(1)}, f32[128,1536]{1,0:T(8,128)}, u32[]{:S(2)}) copy-start(f32[128,1536]{1,0:T(8,128)} %copy-done.12) | copy-start | bytes 2359300
  1279.0 85.2 %copy-start.60 = (f32[1,3072]{1,0:T(1,128)S(1)}, f32[1,3072]{1,0:T(1,128)}, u32[]{:S(2)}) copy-start(f32[1,3072]{1,0:T(1,128)} %copy-done.59) | copy-start | bytes 36868
  1714.7 745.8 %copy-start.122 = (f32[2,12,48]{2,0,1:T(2,128)S(1)}, f32[2,12,48]{2,0,1:T(2,128)}, u32[]{:S(2)}) copy-start(f32[2,12,48]{2,0,1:T(2,128)} %param.36) | copy-start | bytes 13828
  1714.7 745.8 %copy-start.165 = (f32[2,12,48]{2,0,1:T(2,128)S(1)}, f32[2,12,48]{2,0,1:T(2,128)}, u32[]{:S(2)}) copy-start(f32[2,12,48]{2,0,1:T(2,128)} %param.37) | copy-start | bytes 13828
  1714.7 745.8 %copy-start.166 = (f32[2,12,48]{2,0,1:T(2,128)S(1)}, f32[2,12,48]{2,0,1:T(2,128)}, u32[]{:S(2)}) copy-start(f32[2,12,48]{2,0,1:T(2,128)} %param.38) | copy-start | bytes 13828
  (164 other events, 820.7 us)
Sparse Core Ops, SparseCore 0:
  11.7 117.2 all-gather.16
  132.5 70.6 all-gather.18
  206.8 114.2 all-gather.20
  324.5 70.3 all-gather.22
  973.5 741.1 reduce-scatter.4
  1716.9 739.4 reduce-scatter.2
where the time goes:
time: 2490 us; the launch traced here: 2480 us
  waiting for transfers between devices  1090 us (44%)
  blocking collectives  542 us (22%)
  local copies, waits for them, and re-layouts  540 us (22%)
  matrix products  221 us (9%)
  other arithmetic  69.7 us (3%)
    reduce_scatter x2, waiting for transfers between devices, reduce_grads(): lax.psum_scatter(joined, ('fsdp', 'sub'), scatter_dimension=0, tiled=True)  1080 us
    unnamed x409, local copies, waits for them, and re-layouts  206 us
    all_gather x2, blocking collectives, fetch(): lax.all_gather(mat_bc, ('fsdp', 'sub'), axis=0, tiled=True)  137 us
    all_gather x2, blocking collectives, fetch(): lax.all_gather(conv_taps, ('fsdp', 'sub'), axis=0, tiled=True)  134 us
    reshape x12, local copies, waits for them, and re-layouts, reduce_grads(): flat_rows = [grad.reshape(devices, -1) for grad in grads]  122 us
    all_gather x2, blocking collectives, fetch(): lax.all_gather(mat_dt, ('fsdp', 'sub'), axis=0, tiled=True)  120 us
    reshape x2, local copies, waits for them, and re-layouts, reduce_grads(): jnp.pad(joined, ((0, 0), (0, padded - length_all)))  86.9 us
    pad x2, local copies, waits for them, and re-layouts, reduce_grads(): jnp.pad(joined, ((0, 0), (0, padded - length_all)))  78.4 us
  transfers between devices with their start and end apart: 6, of which 2 were waited for; matrix products, arithmetic and copies ran while one was open for 17% of the time, Pallas kernels for 0%

commit v1 on v0

v1 whole, which is shorter than its diff:
```python
from functools import partial

import jax
import jax.numpy as jnp
import numpy as np
from jax import lax
from jax.experimental import pallas as pl
from jax.experimental.pallas import tpu as pltpu
from jax.sharding import PartitionSpec as P

STEP = 10

EPS_NORM = 1e-05
BETA_ONE = 0.9
BETA_TWO = 0.999
ADAM_EPS = 1e-08
RATE_MATRIX = 0.05
RATE_VECTOR = 0.5
RATE_HEADS = 2.0
WEIGHT_DECAY = 0.1

MESH = pl.DeviceIdType.MESH
BF = jnp.bfloat16
F32 = jnp.float32
ANY = pl.BlockSpec(memory_space=pl.ANY)
VMEM = pl.BlockSpec(memory_space=pltpu.VMEM)

WIDTH = 1536
INNER = 3072
STATE = 128
HEADS = 48
LAYERS = 2
WA = 3584
WIN = WA + INNER
PARTS = (
    ("in", 0, 2560, "x"),
    ("in", 2560, 2048, "z"),
    ("in", 4608, 2048, "y"),
    ("out", 0, 512, "x"),
    ("out", 512, 512, "z"),
    ("out", 1024, 512, "y"),
)
BLOCK_ROWS = {"in": 48, "out": 96}
PADDED = {"in": 16, "out": 32}
MATRIX = {"in": (4, 4, 2, 48, WIN), "out": (4, 4, 2, 96, WIDTH)}


def place():
    f = lax.axis_index("fsdp")
    y = lax.axis_index("sub")
    return lax.div(f, 8), lax.rem(lax.div(f, 2), 4), lax.rem(f, 2), y


def device_at(x, z, core, y):
    return (x * 8 + z * 2 + core, y)


def turn(i, by):
    return lax.rem(i + by, 4)


class Wire:
    def __init__(self, send, recv):
        self.send, self.recv, self.copies, self.left_source = send, recv, [], []
        self.x, self.z, self.core, self.y = place()
        x, z, c, y = self.x, self.z, self.core, self.y
        self.partner = device_at(x, z, 1 - c, y)
        self.right = {
            "x": device_at(turn(x, 1), z, c, y),
            "z": device_at(x, turn(z, 1), c, y),
            "y": device_at(x, z, c, turn(y, 1)),
        }
        self.left = {
            "x": device_at(turn(x, 3), z, c, y),
            "z": device_at(x, turn(z, 3), c, y),
            "y": device_at(x, z, c, turn(y, 3)),
        }
        self.index = {"x": x, "z": z, "y": y}

    def greet(self):
        barrier = pltpu.get_barrier_semaphore()
        x, z, c, y = self.x, self.z, self.core, self.y
        peers = [self.partner, device_at(x, z, c, turn(y, 2))]
        peers += list(self.right.values()) + list(self.left.values())
        for peer in peers:
            pl.semaphore_signal(barrier, inc=1, device_id=peer, device_id_type=MESH)
        pl.semaphore_wait(barrier, len(peers))

    def copy(self, src, dst, device):
        number = len(self.copies)
        made = pltpu.make_async_remote_copy(
            src_ref=src,
            dst_ref=dst,
            send_sem=self.send.at[number],
            recv_sem=self.recv.at[number],
            device_id=device,
            device_id_type=MESH,
        )
        made.start()
        self.copies.append(made)
        return made

    def sent(self, made):
        made.wait_send()
        self.left_source.append(made)

    def finish(self):
        for made in self.copies:
            if not any(made is other for other in self.left_source):
                made.wait_send()


def cols(base, j, width, start=0, size=None):
    return pl.ds(pl.multiple_of(base + j * width + start, 128), width if size is None else size)


def dot(left, right):
    return jnp.dot(left, right, preferred_element_type=F32)


def block_half(rows, width):
    if width >= 256:
        first = width // 256 * 128

        def cut(h):
            return (0, rows), {None: (0, width), 0: (0, first), 1: (first, width - first)}[h]
    else:
        first = rows // 32 * 16 if rows % 32 == 0 else rows // 3 * 2

        def cut(h):
            return {None: (0, rows), 0: (0, first), 1: (first, rows - first)}[h], (0, width)
    return cut


def picker(block, pad):
    rows = 4 * block
    pick = np.zeros((rows, 4 * pad), np.float32)
    for r in range(rows):
        pick[r, (r // block) * pad + r % block] = 1.0
    return pick


def gather_regions(part, out, x, z, c, y):
    if part is None:
        half = lambda h: pl.ds(0, 4) if h is None else pl.ds(2 * h, 2)
        one = lambda j, h: None if h == 1 else out.at[x, z, c, j]
        two = lambda j, h: out.at[x, j, c, half(h)]
        three = lambda j, h: out.at[half(h), j, c]
        return (("y", one), ("z", two), ("x", lambda j, h: out.at[j, half(h), c]))
    kind, base, width, last = part
    quarter = width // 4
    half = lambda h: pl.ds(0, 4) if h is None else pl.ds(2 * h, 2)
    full = pl.ds(base, width)
    cut = block_half(BLOCK_ROWS[kind], quarter)

    def block(h, q):
        (row, rows), (col, size) = cut(h)
        return pl.ds(row, rows), cols(base, q, quarter, col, size)

    if last == "x":

        def one(j, h):
            at = block(h, j)
            return out.at[x, z, c, at[0], at[1]]

        def two(j, h):
            size = width if h is None else width // 2
            return out.at[x, j, c, :, pl.ds(base + (h or 0) * size, size)]

        return (("y", one), ("z", two), ("x", lambda j, h: out.at[j, half(h), c, :, full]))
    if last == "z":

        def one(j, h):
            at = block(h, y)
            return out.at[j, z, c, at[0], at[1]]

        two = lambda j, h: out.at[half(h), z, c, :, cols(base, j, quarter)]
        return (("x", one), ("y", two), ("z", lambda j, h: out.at[half(h), j, c, :, full]))

    def one(j, h):
        at = block(h, y)
        return out.at[x, j, c, at[0], at[1]]

    two = lambda j, h: out.at[j, half(h), c, :, cols(base, y, quarter)]
    return (("z", one), ("x", two), ("y", lambda j, h: out.at[half(h), :, c, :, cols(base, j, quarter)]))


class Gather:
    def __init__(self, wire, plans):
        self.wire, self.plans, self.partner = wire, plans, []

    def forward(self, ref):
        self.partner.append(self.wire.copy(ref, ref, self.wire.partner))

    def start(self, phase):
        wire, self.nears = self.wire, []
        for plan in self.plans:
            axis, region = plan[phase]
            own = region(wire.index[axis], None)
            self.nears.append((wire.copy(own, own, wire.right[axis]), wire.copy(own, own, wire.left[axis])))
        if phase == 2:
            for plan in self.plans:
                axis, region = plan[phase]
                self.forward(region(wire.index[axis], None))

    def middle(self, phase):
        wire, self.fars = self.wire, []
        for plan, (to_right, to_left) in zip(self.plans, self.nears):
            axis, region = plan[phase]
            i = wire.index[axis]
            sent = []
            to_right.wait_recv()
            ref = region(turn(i, 3), 0)
            sent.append(wire.copy(ref, ref, wire.right[axis]))
            to_left.wait_recv()
            ref = region(turn(i, 1), 1)
            if ref is not None:
                sent.append(wire.copy(ref, ref, wire.left[axis]))
            self.fars.append(sent)
            if phase == 2:
                self.forward(region(turn(i, 3), None))
                self.forward(region(turn(i, 1), None))

    def end(self, phase):
        for plan, sent in zip(self.plans, self.fars):
            axis, region = plan[phase]
            i = self.wire.index[axis]
            for h, made in enumerate(sent):
                made.wait_recv()
                if phase == 2:
                    self.forward(region(turn(i, 2), h))

    def finish(self):
        for made in self.partner:
            made.wait_recv()


SLOTS = 128
CONVED = INNER + 2 * STATE
DT_AT = CONVED
BLOCK = 512
HIGH = lax.Precision.HIGHEST


def sigmoid(v):
    return 1.0 / (1.0 + jnp.exp(-v))


def dot_t(left, right):
    return lax.dot_general(left, right, (((1,), (1,)), ((), ())), preferred_element_type=F32)


def t_dot(left, right):
    return lax.dot_general(left, right, (((0,), (0,)), ((), ())), preferred_element_type=F32)


def exact(left, right):
    return jnp.dot(left, right, preferred_element_type=F32, precision=HIGH)


def lanes(p, width=128):
    return pl.ds(pl.multiple_of(p * width, width), width)


GATE = 384
COUNTS = {"in": WIN // BLOCK, "out": INNER // GATE}


def weight_block(kind, k):
    if kind == "in":
        return slice(None), lanes(k, BLOCK)
    return lax.div(k, 2), pl.ds(2 * lax.rem(k, 2), 2)


class Weights:
    def __init__(self, hbm, held, out, sems):
        self.hbm, self.held, self.out, self.sems = hbm, held, out, sems

    def copy(self, k):
        at = weight_block("in", k)
        return pltpu.make_async_copy(self.hbm.at[at], self.held.at[at], self.sems.at[k])

    def start(self):
        @pl.loop(0, COUNTS["in"])
        def _(k):
            self.copy(k).start()

    def wait(self, k):
        self.copy(k).wait()

    def get(self, k):
        return self.held[weight_block("in", k)]

    def columns(self, k):
        return self.out[:, :, :, :, lanes(k, BLOCK)].reshape(INNER, BLOCK)

    def again(self, kind, k):
        if kind == "in":
            return self.get(k)
        return self.out[weight_block(kind, k)].reshape(GATE, WIDTH)

    def done(self, kind, k):
        pass


class Stream:
    def __init__(self, hbm, slots, sems):
        self.hbm, self.slots = dict(zip(("in", "out"), hbm)), dict(zip(("in", "out"), slots))
        self.sems = dict(zip(("in", "out"), sems))

    def copy(self, kind, k):
        slot = lax.rem(k, self.slots[kind].shape[0])
        return pltpu.make_async_copy(
            self.hbm[kind].at[weight_block(kind, k)], self.slots[kind].at[slot], self.sems[kind].at[slot]
        )

    def start(self):
        for kind in ("out", "in"):
            for k in range(self.slots[kind].shape[0]):
                self.copy(kind, jnp.int32(k)).start()

    def again(self, kind, k):
        self.copy(kind, k).wait()
        got = self.slots[kind][lax.rem(k, self.slots[kind].shape[0])]
        return got if kind == "in" else got.reshape(GATE, WIDTH)

    def done(self, kind, k):
        count = self.slots[kind].shape[0]

        @pl.when(k + count < COUNTS[kind])
        def _():
            self.copy(kind, k + count).start()


def conv_tile(u, taps, lag):
    total = taps[4:5] + taps[3:4] * u
    for j in (1, 2, 3):
        total = total + taps[3 - j : 4 - j] * (pltpu.roll(u, j, 0) * lag[:, j : j + 1])
    return total


def conv_back(d_cv, u, taps, lag):
    d_u = taps[3:4] * d_cv
    rows = [None] * 5
    rows[4] = jnp.sum(d_cv, axis=0, keepdims=True)
    rows[3] = jnp.sum(d_cv * u, axis=0, keepdims=True)
    for j in (1, 2, 3):
        kept = d_cv * lag[:, j : j + 1]
        rows[3 - j] = jnp.sum(kept * pltpu.roll(u, j, 0), axis=0, keepdims=True)
        d_u = d_u + taps[3 - j : 4 - j] * pltpu.roll(kept, SLOTS - j, 0)
    return d_u, rows


def silu_slope(v):
    s = sigmoid(v)
    return s * (1.0 + v * (1.0 - s))


def triangle(lower):
    t = lax.broadcasted_iota(jnp.int32, (SLOTS, SLOTS), 0)
    s = lax.broadcasted_iota(jnp.int32, (SLOTS, SLOTS), 1)
    return jnp.where((s <= t) if lower else (s >= t), 1.0, 0.0).astype(F32)


def lane_index():
    return lax.broadcasted_iota(jnp.int32, (SLOTS, SLOTS), 1)


class Layer:
    def __init__(self, layer, **refs):
        self.layer = layer
        self.__dict__.update(refs)

    def taps(self, at):
        return self.rows[self.layer, :, at]

    def gain_in(self):
        return self.rows[self.layer, 5:6, :WIDTH]

    def gain_gate(self, k, width):
        return self.rows[self.layer, 5:6, pl.ds(pl.multiple_of(WIDTH + k * width, 128), width)]

    def head_rows(self):
        return self.heads[self.layer]


def pair_row(row, k=0):
    first = lax.broadcasted_iota(jnp.int32, (1, 128), 1) < 64
    return jnp.where(first, row[:, 2 * k : 2 * k + 1], row[:, 2 * k + 1 : 2 * k + 2])


def step_sizes(m):
    pre = m.pa[:, DT_AT : DT_AT + 128] + m.head_rows()[0:1]
    step = jnp.maximum(pre, 0.0) + jnp.log1p(jnp.exp(-jnp.abs(pre)))
    rate = -jnp.exp(m.head_rows()[1:2])
    m.step[...] = step
    level = exact(triangle(True), step * rate)
    m.level[...] = level
    m.level_t[...] = level.T


def states(m):
    cv = m.cv[:, INNER:CONVED]
    act = cv * sigmoid(cv)
    low = act.astype(BF)
    m.state_in[...] = low[:, :STATE]
    m.state_out[...] = low[:, STATE:]
    m.inner[...] = dot_t(low[:, STATE:], low[:, :STATE])


def group_columns(m, g):
    shift = lax.rem(SLOTS - 8 * g, SLOTS)
    return (
        pltpu.roll(m.level[...], shift, 1),
        pltpu.roll(m.step[...], shift, 1),
        m.level_t[pl.ds(pl.multiple_of(8 * g, 8), 8), :],
        pltpu.roll(m.head_rows(), shift, 1)[2:3],
    )


def pair_columns(m, p):
    shift = lax.rem(SLOTS - 2 * p, SLOTS)
    rows = [m.level_t[pl.ds(2 * p + e, 1), :] for e in (0, 1)]
    return (
        pltpu.roll(m.level[...], shift, 1),
        pltpu.roll(m.step[...], shift, 1),
        rows,
        pair_row(pltpu.roll(m.head_rows(), shift, 1)[2:3]),
    )


def nothing():
    pass


def forward(m, weights, halfway=nothing, mixed=nothing, gated=nothing, turned=nothing):
    r = m.resid[...]
    scale = lax.rsqrt(jnp.sum(r * r, axis=1, keepdims=True) * (1.0 / WIDTH) + EPS_NORM)
    live = m.lag[:, 0:1]
    m.normed[...] = (r * scale * m.gain_in()).astype(BF) * live.astype(BF)

    @pl.loop(0, WA // BLOCK)
    def _(k):
        weights.wait(k)
        m.pa[:, lanes(k, BLOCK)] = dot(m.normed[...], weights.get(k))

    step_sizes(m)
    lag = m.lag[...]
    m.cv[:, INNER:CONVED] = conv_tile(m.pa[:, INNER:CONVED], m.taps(slice(INNER, CONVED)), lag)
    states(m)

    @pl.loop(0, INNER // BLOCK)
    def _(k):
        weights.wait(WA // BLOCK + k)
        m.px[:, lanes(k, BLOCK)] = dot(m.normed[...], weights.get(WA // BLOCK + k))

    m.square[...] = jnp.zeros((SLOTS, 128), F32)

    def heads(g):
        level, step, rows, skips = group_columns(m, g)
        first = lane_index() < 64
        for k in range(4):
            at = lanes(4 * g + k)
            cv = conv_tile(m.px[:, at], m.taps(at), m.lag[...])
            m.cv[:, at] = cv
            act = cv * sigmoid(cv)
            both = jnp.where(first, step[:, 2 * k : 2 * k + 1], step[:, 2 * k + 1 : 2 * k + 2])
            scaled = act * both
            mixes = []
            for h in (2 * k, 2 * k + 1):
                decay = jnp.exp(level[:, h : h + 1] - rows[h : h + 1] + m.mask[...])
                mixes.append((m.inner[...] * decay).astype(BF))
            right = jnp.concatenate(
                [jnp.where(first, scaled, 0.0).astype(BF), jnp.where(first, 0.0, scaled).astype(BF)], axis=0
            )
            y = dot(jnp.concatenate(mixes, axis=1), right) + act * pair_row(skips, k)
            m.y[:, at] = y
            z = m.pa[:, at]
            gated = y * (z * sigmoid(z))
            m.work[:, at] = gated
            m.square[...] += gated * gated

    pl.loop(0, 3)(heads)
    halfway()
    pl.loop(3, 6)(heads)
    mixed()
    scale = lax.rsqrt(jnp.sum(m.square[...], axis=1, keepdims=True) * (1.0 / INNER) + EPS_NORM)
    m.gate_scale[...] = jnp.broadcast_to(scale, (SLOTS, 128))

    @pl.loop(0, INNER // BLOCK)
    def _(k):
        at = lanes(k, BLOCK)
        m.gate_low[:, at] = (m.work[:, at] * m.gate_scale[:, 0:1] * m.gain_gate(k, BLOCK)).astype(BF)

    gated()
    transposes(m)
    turned()

    @pl.loop(0, WIDTH // BLOCK)
    def _(k):
        at = lanes(k, BLOCK)
        branch = dot(m.gate_low[...], weights.columns(k))
        m.resid_out[:, at] = m.resid[:, at] + m.lag[:, 0:1] * branch


def transposes(m):
    @pl.loop(0, WIDTH // 128)
    def _(k):
        m.normed_t[lanes(k), :] = m.normed[:, lanes(k)].T

    @pl.loop(0, INNER // 128)
    def _(k):
        m.gate_t[lanes(k), :] = m.gate_low[:, lanes(k)].T


def branch_grad(m):
    m.d_c[...] = (m.upstream[...] * m.lag[:, 0:1]).astype(BF)


def backward(m, weights):
    m.square[...] = jnp.zeros((SLOTS, 128), F32)

    @pl.loop(0, COUNTS["out"])
    def _(k):
        at = lanes(k, GATE)
        d_gate = dot_t(m.d_c[...], weights.again("out", k))
        weights.done("out", k)
        m.work[:, at] = d_gate
        z = m.pa[:, at]
        hat = m.y[:, at] * (z * sigmoid(z)) * m.gate_scale[:, 0:1]
        m.grad_rows[5:6, pl.ds(pl.multiple_of(WIDTH + k * GATE, 128), GATE)] = jnp.sum(
            d_gate * hat, axis=0, keepdims=True
        )
        both = d_gate * m.gain_gate(k, GATE) * hat
        m.square[...] += both[:, :128] + both[:, 128:256] + both[:, 256:]

    m.square[...] = jnp.broadcast_to(
        jnp.sum(m.square[...], axis=1, keepdims=True) * (1.0 / INNER), (SLOTS, 128)
    )
    m.grad_heads[...] = jnp.zeros((8, 128), F32)
    m.d_inner[...] = jnp.zeros((SLOTS, 128), F32)
    m.d_level[...] = jnp.zeros((SLOTS, 128), F32)
    m.d_level_t[...] = jnp.zeros((SLOTS, 128), F32)
    m.d_step[...] = jnp.zeros((SLOTS, 128), F32)

    yield

    def heads(p):
        level, step, rows, skip = pair_columns(m, p)
        index = lane_index()
        first = index < 64
        at = lanes(p)
        z = m.pa[:, at]
        s = sigmoid(z)
        z_gate = z * s
        y = m.y[:, at]
        scale = m.gate_scale[...]
        hat = y * z_gate * scale
        d_gated = scale * (m.work[:, at] * m.gain_gate(p, 128) - hat * m.square[...])
        d_y = d_gated * z_gate
        d_z = d_gated * y * (s * (1.0 + z * (1.0 - s)))
        m.d_in[:, at] = d_z.astype(BF)
        cv = m.cv[:, at]
        s = sigmoid(cv)
        act = cv * s
        both = jnp.where(first, step[:, 0:1], step[:, 1:2])
        scaled = (act * both).astype(BF)
        d_ssd = jnp.concatenate(
            [jnp.where(first, d_y, 0.0).astype(BF), jnp.where(first, 0.0, d_y).astype(BF)], axis=0
        )
        d_mix = dot_t(d_ssd, scaled)
        mixes, sums = [], []
        for e in (0, 1):
            decay = jnp.exp(level[:, e : e + 1] - rows[e] + m.mask[...])
            mix = m.inner[...] * decay
            mixes.append(mix.astype(BF))
            one = d_mix[SLOTS * e : SLOTS * (e + 1)]
            m.d_inner[...] += one * decay
            gap = one * mix
            sums.append(jnp.sum(gap, axis=1, keepdims=True))
            m.d_level_t[pl.ds(2 * p + e, 1), :] = jnp.sum(gap, axis=0, keepdims=True)
        m.d_level[...] = jnp.where(index == 2 * p, sums[0], jnp.where(index == 2 * p + 1, sums[1], m.d_level[...]))
        d_scaled = t_dot(jnp.concatenate(mixes, axis=0), d_ssd)
        back = d_scaled * act
        one = jnp.sum(jnp.where(first, back, 0.0), axis=1, keepdims=True)
        two = jnp.sum(jnp.where(first, 0.0, back), axis=1, keepdims=True)
        m.d_step[...] = jnp.where(index == 2 * p, one, jnp.where(index == 2 * p + 1, two, m.d_step[...]))
        row = jnp.sum(d_y * act, axis=0, keepdims=True)
        one = jnp.sum(jnp.where(first[:1], row, 0.0), axis=1, keepdims=True)
        two = jnp.sum(jnp.where(first[:1], 0.0, row), axis=1, keepdims=True)
        m.grad_heads[2:3] = jnp.where(
            index[:1] == 2 * p, one, jnp.where(index[:1] == 2 * p + 1, two, m.grad_heads[2:3])
        )
        d_cv = (d_scaled * both + d_y * skip) * (s * (1.0 + cv * (1.0 - s)))
        d_u, grads = conv_back(d_cv, m.px[:, at], m.taps(at), m.lag[...])
        m.d_in[:, lanes(WA // 128 + p)] = d_u.astype(BF)
        for n in range(5):
            m.grad_rows[n : n + 1, at] = grads[n]

    pl.loop(0, HEADS // 4)(heads)
    yield
    pl.loop(HEADS // 4, HEADS // 2)(heads)
    yield

    d_inner = m.d_inner[...].astype(BF)
    d_out = dot(d_inner, m.state_in[...])
    d_in = t_dot(d_inner, m.state_out[...])
    for n, d_state in enumerate((d_in, d_out)):
        at = slice(INNER + STATE * n, INNER + STATE * (n + 1))
        d_cv = d_state * silu_slope(m.cv[:, at])
        d_u, grads = conv_back(d_cv, m.pa[:, at], m.taps(at), m.lag[...])
        m.d_in[:, at] = d_u.astype(BF)
        for k in range(5):
            m.grad_rows[k : k + 1, at] = grads[k]

    rate = -jnp.exp(m.head_rows()[1:2])
    run = exact(triangle(False), m.d_level[...] - m.d_level_t[...].T)
    d_step = m.d_step[...] + run * rate
    pre = m.pa[:, DT_AT : DT_AT + 128] + m.head_rows()[0:1]
    d_dt = d_step * sigmoid(pre)
    m.d_in[:, DT_AT : DT_AT + 128] = d_dt.astype(BF)
    m.d_in[:, DT_AT + 128 : WA] = jnp.zeros((SLOTS, WA - DT_AT - 128), BF)
    m.grad_heads[0:1] = jnp.sum(d_dt, axis=0, keepdims=True)
    m.grad_heads[1:2] = jnp.sum(run * m.step[...], axis=0, keepdims=True) * rate

    yield
    m.d_normed[...] = jnp.zeros((SLOTS, WIDTH), F32)

    @pl.loop(0, COUNTS["in"])
    def _(k):
        m.d_normed[...] += dot_t(m.d_in[:, lanes(k, BLOCK)], weights.again("in", k))
        weights.done("in", k)

    yield
    d_normed = m.d_normed[...] * m.lag[:, 0:1]
    r = m.resid[...].astype(F32)
    scale = lax.rsqrt(jnp.sum(r * r, axis=1, keepdims=True) * (1.0 / WIDTH) + EPS_NORM)
    hat = r * scale
    m.grad_rows[5:6, :WIDTH] = jnp.sum(d_normed * hat, axis=0, keepdims=True)
    d_hat = d_normed * m.gain_in()
    mean = jnp.sum(d_hat * hat, axis=1, keepdims=True) * (1.0 / WIDTH)
    m.upstream_out[...] = m.upstream[...] + scale * (d_hat - hat * mean)
    share_small(m)


def device_of(d):
    f, y = divmod(d, 4)
    return f // 8, f // 2 % 4, f % 2, y


def share_small(m):
    lane = lax.broadcasted_iota(jnp.int32, (8, 128), 1)
    row = lax.broadcasted_iota(jnp.int32, (8, 128), 0)
    heads = m.grad_heads[...]
    last = jnp.where(
        row == 6,
        jnp.where(lane < 64, heads[0:1], pltpu.roll(heads, 64, 1)[2:3]),
        heads[1:2],
    )

    def window(start, size):
        block, off = divmod(start, 128)
        tile = m.grad_rows[:, 128 * block : 128 * (block + 1)]
        if off + size > 128:
            tile = jnp.where(lane >= off, tile, m.grad_rows[:, 128 * (block + 1) : 128 * (block + 2)])
        return tile

    for d in range(128):
        tile = jnp.where(row < 5, window(26 * d, 26), window(36 * d, 36))
        m.shares[device_of(d)] = jnp.where(row < 6, tile, last)


PARAMS = ("mask", "lag", "rows", "heads")
ROWS_SHAPE = (LAYERS, 8, 4608)
HEADS_SHAPE = (LAYERS, 8, 128)
KEPT = (("pa", (SLOTS, WA), F32), ("px", (SLOTS, INNER), F32), ("cv", (SLOTS, CONVED), F32),
        ("y", (SLOTS, INNER), F32), ("gate_scale", (SLOTS, 128), F32))
OPERANDS = (("normed_t", (WIDTH, SLOTS), BF), ("gate_t", (INNER, SLOTS), BF))
RESULT = (("resid_out", (SLOTS, WIDTH), F32),)
GRADS = (("upstream_out", (SLOTS, WIDTH), F32), ("d_in", (SLOTS, WIN), BF), ("d_c", (SLOTS, WIDTH), BF), ("shares", (4, 4, 2, 4, 8, 128), F32))
SMALL = tuple((name, (SLOTS, 128), F32) for name in ("step", "level", "level_t", "inner", "square"))
STATES = (("state_in", (SLOTS, 128), BF), ("state_out", (SLOTS, 128), BF))
WORK = (("work", (SLOTS, INNER), F32),)
LOW = (("normed", (SLOTS, WIDTH), BF), ("gate_low", (SLOTS, INNER), BF))
BACK = tuple((name, (SLOTS, 128), F32) for name in ("d_inner", "d_level", "d_level_t", "d_step")) + (
    ("d_normed", (SLOTS, WIDTH), F32),
    ("grad_rows", (8, 4608), F32),
    ("grad_heads", (8, 128), F32),
)


class Phase:
    def __init__(self, wire, axis, half, tiles, index, term, refs):
        self.wire, self.axis, self.i = wire, axis, wire.index[axis]
        self.half, self.tiles, self.index, self.term = half, tiles, index, term
        self.opp, self.mid, self.from_left, self.from_right, self.acc = refs
        self.kind = self.opp.dtype

    def each(self, h, body):
        count = self.tiles[h]
        if count <= 2:
            for t in range(count):
                body(self.index(h, t), t)
        else:

            @pl.loop(0, count)
            def _(t):
                body(self.index(h, t), t)

    def device(self, h):
        return (self.wire.right if h == 0 else self.wire.left)[self.axis]

    def start(self):
        j = turn(self.i, 2)
        self.mids = [None, None]
        for h in (0, 1):
            if self.tiles[h]:

                def body(at, t, h=h):
                    self.opp[at] = self.term(j, h, t).astype(self.kind)

                self.each(h, body)
                part = self.half(h)
                self.mids[h] = self.wire.copy(self.opp.at[part], self.mid.at[part], self.device(h))

    def near(self):
        self.nears = []
        for h in (0, 1):
            if self.tiles[h]:
                self.mids[h].wait_recv()
                j = turn(self.i, 1 if h == 0 else 3)

                def body(at, t, h=h, j=j):
                    self.mid[at] = (self.term(j, h, t) + self.mid[at].astype(F32)).astype(self.kind)

                self.each(h, body)
                part = self.half(h)
                land = self.from_left if h == 0 else self.from_right
                self.nears.append(self.wire.copy(self.mid.at[part], land.at[part], self.device(h)))

    def alone(self):
        for h in (0, 1):
            if self.tiles[h]:
                self.wire.sent(self.mids[h])
                j = turn(self.i, 3 if h == 0 else 1)

                def body(at, t, h=h, j=j):
                    self.opp[at] = self.term(j, h, t).astype(self.kind)

                self.each(h, body)
                part = self.half(h)
                land = self.from_right if h == 0 else self.from_left
                self.nears.append(self.wire.copy(self.opp.at[part], land.at[part], self.device(1 - h)))

    def end(self):
        for made in self.nears:
            made.wait_recv()
        for h in (0, 1):

            def body(at, t, h=h):
                total = self.term(self.i, h, t) + self.from_left[at].astype(F32) + self.from_right[at].astype(F32)
                self.acc[at] = total.astype(self.acc.dtype)

            self.each(h, body)


def slab_shapes(part):
    if part is None:
        return ((4, 4, 8, 128), (4, 8, 128), (8, 128))
    kind, _, width, first = part
    rows, quarter = BLOCK_ROWS[kind], width // 4
    if first == "x":
        return ((4, rows, width), (rows, width), (rows, quarter))
    if first == "z":
        return ((4, rows, width), (4, rows, quarter), (rows, quarter))
    return ((4, 4, rows, quarter), (4, rows, quarter), (rows, quarter))


def pair(h):
    return pl.ds(2 * h, 2)


def part_phases(wire, part, left, right, bufs):
    kind, base, width, first = part
    rows, quarter = BLOCK_ROWS[kind], width // 4
    accs = [item[4] for item in bufs]
    every = slice(None)
    tile = 512 if kind == "in" else 256
    cut = block_half(rows, quarter)

    def block(h):
        (row, count), (col, size) = cut(h)
        return pl.ds(row, count), pl.ds(col, size)

    last_axis = {"x": "y", "z": "x", "y": "z"}[first]

    def last_term(j, h, t):
        at = block(h)
        if first == "x":
            (row, count), (col, size) = cut(h)
            return accs[1][pl.ds(row, count), cols(0, j, quarter, col, size)]
        return accs[1][j, at[0], at[1]]

    last = Phase(wire, last_axis, block, (1, 1), lambda h, t: block(h), last_term, bufs[2])
    if first in "xz":
        step = lambda t: pl.multiple_of(t * tile, tile)

        def one_term(j, h, t):
            lhs = left[j, pair(h)] if first == "x" else left[pair(h), j]
            rhs = right[:, pl.ds(pl.multiple_of(base + t * tile, tile), tile)]
            return dot(lhs.reshape(2 * rows, 256), rhs).reshape(2, rows, tile)

        one = Phase(
            wire, first, lambda h: (pair(h),), (width // tile,) * 2,
            lambda h, t: (pair(h), every, pl.ds(step(t), tile)), one_term, bufs[0],
        )
    else:

        def one_term(j, h, t):
            lhs = left[2 * h + lax.div(t, 2), pl.ds(2 * lax.rem(t, 2), 2)]
            return dot(lhs.reshape(2 * rows, 256), right[:, cols(base, j, quarter)]).reshape(2, rows, quarter)

        one = Phase(
            wire, "y", lambda h: (pair(h),), (4, 4),
            lambda h, t: (2 * h + lax.div(t, 2), pl.ds(2 * lax.rem(t, 2), 2)), one_term, bufs[0],
        )
    if first == "x":
        half = width // 2
        count = 1 if half < 1024 else 2
        size = half // count
        two = Phase(
            wire, "z", lambda h: (every, pl.ds(half * h, half)), (count, count),
            lambda h, t: (every, pl.ds(half * h + size * t, size)),
            lambda j, h, t: accs[0][j, :, pl.ds(half * h + size * t, size)].astype(F32), bufs[1],
        )
    elif first == "z":
        two = Phase(
            wire, "y", lambda h: (pair(h),), (2, 2), lambda h, t: (2 * h + t,),
            lambda j, h, t: accs[0][2 * h + t, :, cols(0, j, quarter)].astype(F32), bufs[1],
        )
    else:
        two = Phase(
            wire, "x", lambda h: (pair(h),), (2, 2), lambda h, t: (2 * h + t,),
            lambda j, h, t: accs[0][j, 2 * h + t].astype(F32), bufs[1],
        )
    return one, two, last


def small_phases(wire, own, far, bufs):
    accs = [item[4] for item in bufs]
    rows = lambda h: (pair(h),)
    at = lambda h, t: (2 * h + t,)
    return (
        Phase(wire, "y", rows, (2, 2), at, lambda j, h, t: own[2 * h + t, :, j] + far[2 * h + t, :, j], bufs[0]),
        Phase(wire, "x", rows, (2, 2), at, lambda j, h, t: accs[0][j, 2 * h + t], bufs[1]),
        Phase(
            wire, "z", lambda h: (pl.ds(0, 8),), (1, 0), lambda h, t: (pl.ds(0, 8),),
            lambda j, h, t: accs[1][j], bufs[2],
        ),
    )


class Reduce:
    def __init__(self, wire, parts, phases, pads, outs, picks):
        self.wire, self.parts, self.phases = wire, parts, phases
        self.pads, self.outs, self.picks, self.arrived = pads, outs, picks, []

    def start(self):
        for phases in self.phases:
            phases[0].start()

    def near(self, step):
        for phases in self.phases:
            phases[step].near()
        for phases in self.phases:
            phases[step].alone()

    def turn(self, step):
        for phases in self.phases:
            phases[step].end()
            phases[step + 1].start()

    def scatter(self):
        wire, y = self.wire, self.wire.y
        for part, phases, pad, out in zip(self.parts, self.phases, self.pads, self.outs):
            phases[2].end()
            if part is None:
                out[...] = phases[2].acc[...]
                continue
            low = phases[2].acc[...].astype(BF)
            pad[...] = dot(self.picks[part[0]][...], low).astype(BF).reshape(pad.shape)
            self.arrived += [
                wire.copy(pad.at[turn(y, by)], out.at[y], device_at(wire.x, wire.z, wire.core, turn(y, by)))
                for by in (1, 3, 2)
            ]
            out[y] = pad[y]

    def finish(self):
        for made in self.arrived:
            made.wait_recv()


def sum_shapes(parts):
    return [
        jax.ShapeDtypeStruct((4, PADDED[part[0]], part[2] // 4), BF) if part else jax.ShapeDtypeStruct((8, 128), F32)
        for part in parts
    ]


def ring_scratch(parts):
    scratch = []
    for part in parts:
        low = BF if part else F32
        for n, shape in enumerate(slab_shapes(part)):
            scratch += [pltpu.VMEM(shape, low)] * 4 + [pltpu.VMEM(shape, F32 if n else low)]
    return scratch + [pltpu.VMEM(shape.shape, shape.dtype) for shape in sum_shapes(parts)]


def take_ring(take, parts):
    return [[take(5) for _ in range(3)] for _ in parts], take(len(parts))


class Swap:
    def __init__(self, wire, src, dst, far_src, far_dst, sem):
        self.here = pltpu.make_async_copy(src, dst, sem)
        self.here.start()
        self.there = wire.copy(far_src, far_dst, wire.partner)

    def wait(self):
        self.here.wait()
        self.there.wait_recv()


def swap_rows(wire, ref, both, sem):
    c = wire.core
    return Swap(
        wire, ref.at[:, :, c], both.at[:, :, :, pl.ds(0, 128)],
        ref.at[:, :, 1 - c], both.at[:, :, :, pl.ds(128, 128)], sem,
    )


def swap_tokens(wire, ref, both, sem):
    return Swap(wire, ref, both.at[pl.ds(0, 128), :], ref, both.at[pl.ds(128, 128), :], sem)


IN_PARTS, OUT_PARTS = PARTS[:3], PARTS[3:]
BOTH = {"in": [(4, 4, 48, 256), (256, WIN)], "out": [(4, 4, 96, 256), (256, WIDTH)]}
PICKS = [(64, 48), (128, 96)]


def picks():
    return jnp.asarray(picker(12, 16).T, BF), jnp.asarray(picker(24, 32).T, BF)


def call_params(number):
    return pltpu.CompilerParams(collective_id=number, has_side_effects=True, vmem_limit_bytes=62 * 2**20)


def copies_of(parts):
    return sum(18 + 3 * (part is not None) for part in parts)


def sems(copies, local):
    return [pltpu.SemaphoreType.DMA((n,)) for n in (copies, copies, local)]


def last_layer(weights, params, inputs):
    ins = PARAMS + tuple(key for key, _ in inputs)
    outs = RESULT + OPERANDS + GRADS
    temps = KEPT + LOW + SMALL + STATES + WORK + BACK

    def kernel(*refs):
        refs = list(refs)
        take = lambda n: [refs.pop(0) for _ in range(n)]
        in_hbm, out_hbm = take(2)
        named = {key: refs.pop(0) for key in ins}
        named.update({entry[0]: refs.pop(0) for entry in outs + temps})
        held_in, held_out = take(2)
        block_sems, send, recv, local = take(4)
        wire = Wire(send, recv)
        m = Layer(LAYERS - 1, **named)
        moving = Weights(in_hbm, held_in, held_out, block_sems)
        moving.start()
        x, z, c, y = wire.x, wire.z, wire.core, wire.y
        plans = [gather_regions(part, held_out, x, z, c, y) for part in OUT_PARTS]
        sources = [gather_regions(part, out_hbm, x, z, c, y) for part in OUT_PARTS]
        placed = []
        for n, (plan, source) in enumerate(zip(plans, sources)):
            axis, region = plan[2]
            own = wire.index[axis]
            placed.append(pltpu.make_async_copy(source[2][1](own, None), region(own, None), local.at[n]))
            placed[n].start()
        wire.greet()
        for made in placed:
            made.wait()
        gather = Gather(wire, plans)
        gather.start(2)

        forward(
            m, moving, halfway=lambda: gather.middle(2), gated=lambda: gather.end(2), turned=gather.finish
        )
        branch_grad(m)
        for _ in backward(m, moving):
            pass
        wire.finish()

    made = pl.pallas_call(
        kernel,
        out_shape=[jax.ShapeDtypeStruct(shape, kind) for _, shape, kind in outs],
        in_specs=[ANY] * 2 + [VMEM] * len(ins),
        out_specs=[VMEM] * len(outs),
        scratch_shapes=[pltpu.VMEM(shape, kind) for _, shape, kind in temps]
        + [pltpu.VMEM((WIDTH, WIN), BF), pltpu.VMEM(MATRIX["out"], BF)]
        + [pltpu.SemaphoreType.DMA((COUNTS["in"],))]
        + sems(3 * 9, 3),
        compiler_params=call_params(3),
        name="forward_backward_last",
    )(*weights, *[params[key] for key in PARAMS], *[value for _, value in inputs])
    return {entry[0]: value for entry, value in zip(outs, made)}


SLOT_SHAPES = [(3, WIDTH, BLOCK), (3, 2, 2, 96, WIDTH)]
ALL_PARTS = PARTS + (None,)


def reduce_layer(name, number, grads, weights=(), params=None, inputs=()):
    ins = (PARAMS + tuple(key for key, _ in inputs)) if weights else ()
    results = GRADS if weights else ()
    temps = SMALL + STATES + WORK + BACK if weights else ()
    count = len(ALL_PARTS)

    def kernel(*refs):
        refs = list(refs)
        take = lambda n: [refs.pop(0) for _ in range(n)]
        p48, p96, n_in, d_in, g_in, dc_in, s_in = take(7)
        hbm = take(len(weights))
        named = {key: refs.pop(0) for key in ins}
        sums = take(count)
        named.update({entry[0]: refs.pop(0) for entry in results + temps})
        n2, d2, g2, dc2, s_own, s_far = take(6)
        bufs, pads = take_ring(take, ALL_PARTS)
        slots, slot_sems = (take(2), take(2)) if weights else ([], [])
        send, recv, local = take(3)
        wire = Wire(send, recv)
        c = wire.core
        if weights:
            m = Layer(0, **named)
            moving = Stream(hbm, slots, slot_sems)
            moving.start()
        wire.greet()
        swaps = [
            swap_rows(wire, g_in, g2, local.at[0]),
            swap_tokens(wire, dc_in, dc2, local.at[1]),
            swap_rows(wire, n_in, n2, local.at[2]),
            *[
                swap_tokens(wire, d_in.at[:, pl.ds(base, width)], d2.at[:, pl.ds(base, width)], local.at[n + 3])
                for n, (_, base, width, _) in enumerate(IN_PARTS)
            ],
            Swap(wire, s_in.at[:, :, c], s_own, s_in.at[:, :, 1 - c], s_far, local.at[6]),
        ]
        operands = {"in": (n2, d2), "out": (g2, dc2)}
        phases = [part_phases(wire, part, *operands[part[0]], bufs[n]) for n, part in enumerate(PARTS)]
        phases.append(small_phases(wire, s_own, s_far, bufs[count - 1]))
        choose = {"in": p48, "out": p96}
        cut = len(IN_PARTS)
        out = Reduce(wire, OUT_PARTS, phases[cut:-1], pads[cut:-1], sums[cut:-1], choose)
        rest = phases[:cut] + phases[-1:]
        rest = Reduce(
            wire, IN_PARTS + (None,), rest, pads[:cut] + pads[-1:], sums[:cut] + sums[-1:], choose
        )
        if weights:
            branch_grad(m)
            step_sizes(m)
            states(m)
        stages = backward(m, moving) if weights else iter(())
        for swap in swaps[:2]:
            swap.wait()
        out.start()
        swaps[2].wait()
        for swap, item in zip(swaps[3:6], phases):
            swap.wait()
            item[0].start()
        swaps[6].wait()
        phases[-1][0].start()
        next(stages, None)
        next(stages, None)
        out.near(0)
        rest.near(0)
        for _ in stages:
            pass
        out.turn(0)
        rest.turn(0)
        out.near(1)
        rest.near(1)
        out.turn(1)
        rest.turn(1)
        out.near(2)
        rest.near(2)
        out.scatter()
        rest.scatter()
        out.finish()
        rest.finish()
        wire.finish()

    out_shape = sum_shapes(ALL_PARTS)
    out_shape += [jax.ShapeDtypeStruct(shape, kind) for _, shape, kind in results]
    scratch = [pltpu.VMEM(shape, kind) for _, shape, kind in temps]
    scratch += [pltpu.VMEM(shape, BF) for shape in BOTH["in"] + BOTH["out"]]
    scratch += [pltpu.VMEM((4, 4, 4, 8, 128), F32)] * 2
    scratch += ring_scratch(ALL_PARTS)
    if weights:
        scratch += [pltpu.VMEM(shape, BF) for shape in SLOT_SHAPES]
        scratch += [pltpu.SemaphoreType.DMA((shape[0],)) for shape in SLOT_SHAPES]
    made = pl.pallas_call(
        kernel,
        out_shape=out_shape,
        in_specs=[VMEM] * 2 + [ANY] * (5 + len(weights)) + [VMEM] * len(ins),
        out_specs=[VMEM] * len(out_shape),
        scratch_shapes=scratch + sems(7 + copies_of(ALL_PARTS), 7),
        compiler_params=call_params(number),
        name=name,
    )(
        *picks(),
        grads["normed_t"].reshape(4, 4, 2, 48, 128),
        grads["d_in"],
        grads["gate_t"].reshape(4, 4, 2, 96, 128),
        grads["d_c"],
        grads["shares"],
        *weights,
        *([params[key] for key in PARAMS] if weights else []),
        *[value for _, value in inputs],
    )
    return made[:count], {entry[0]: value for entry, value in zip(results, made[count:])}


class Held:
    def __init__(self, refs):
        self.refs = refs

    def wait(self, k):
        pass

    def get(self, k):
        return self.refs["in"][:, :, :, :, lanes(k, BLOCK)].reshape(WIDTH, BLOCK)

    def columns(self, k):
        return self.refs["out"][:, :, :, :, lanes(k, BLOCK)].reshape(INNER, BLOCK)


def own_masks(lengths, owners, device, mask, lag):
    spots = lax.broadcasted_iota(jnp.int32, (1, 256), 1).astype(F32)
    length = lengths[...].astype(F32)
    hit = owners[...] == device
    earliest = jnp.min(jnp.where(hit, spots, 1e6), axis=1, keepdims=True)
    one = jnp.sum(jnp.where(hit & (spots == earliest), length, 0.0), axis=1, keepdims=True)
    two = jnp.sum(jnp.where(hit, length, 0.0), axis=1, keepdims=True)

    def segment(at):
        return jnp.where(at < one, 0.0, jnp.where(at < two, 1.0, 2.0))

    t = lax.broadcasted_iota(jnp.int32, (SLOTS, SLOTS), 0).astype(F32)
    s = lax.broadcasted_iota(jnp.int32, (SLOTS, SLOTS), 1).astype(F32)
    mask[...] = jnp.where((s <= t) & (segment(s) == segment(t)), 0.0, -1e30)
    same = jnp.where((t >= s) & (segment(t - s) == segment(t)), 1.0, 0.0)
    lag[...] = jnp.where(s == 0.0, jnp.where(t < two, 1.0, 0.0), same)


def small_tile(conv, gain, device):
    row = lax.broadcasted_iota(jnp.int32, (16, 128), 0)
    taps = jnp.zeros((16, 128), F32)
    norms = jnp.zeros((16, 128), F32)
    for layer in range(LAYERS):
        for k in range(5):
            line = jnp.pad(conv[k, layer : layer + 1, :], ((0, 0), (0, 102)))
            taps = jnp.where(row == 8 * layer + k, line, taps)
        line = jnp.pad(gain[layer : layer + 1, :], ((0, 0), (0, 92)))
        norms = jnp.where(row == 8 * layer + 5, line, norms)
    taps = pltpu.roll(taps, lax.rem(26 * device, 128), 1)
    norms = pltpu.roll(norms, lax.rem(36 * device, 128), 1)
    return jnp.where(lax.rem(row, 8) == 5, norms, taps).astype(BF)


def unpack_small(tiles, rows):
    lane = lax.broadcasted_iota(jnp.int32, (16, 128), 1)
    row = lax.rem(lax.broadcasted_iota(jnp.int32, (16, 128), 0), 8)

    def block(b, size):
        total = None
        for d in range(128):
            start, end = size * d - 128 * b, size * (d + 1) - 128 * b
            if end <= 0 or start >= 128:
                continue
            tile = tiles[device_of(d)].astype(F32)
            total = tile if total is None else jnp.where(lane >= start, tile, total)
        return total

    for b in range(36):
        total = block(b, 36)
        if b < 26:
            total = jnp.where(row == 5, total, block(b, 26))
        at = slice(128 * b, 128 * (b + 1))
        rows[0, :, at] = total[:8]
        rows[1, :, at] = total[8:]


def prepare_rows(refs, layer, row_in, ins):
    inner, state, step, out = refs
    row_in[...] = jnp.zeros(row_in.shape, F32)
    for r in range(12):
        at = slice(r, r + 1)
        row_in[at, :INNER] = inner[r, layer : layer + 1, :INNER]
        row_in[at, INNER:CONVED] = state[r, layer : layer + 1, :]
        row_in[at, DT_AT : DT_AT + HEADS] = step[r, layer : layer + 1, :]
        row_in[at, WA:] = inner[r, layer : layer + 1, INNER:]
    for (kind, base, width, _), ref in zip(PARTS, ins):
        for q in range(4):
            at = slice(base + q * width // 4, base + (q + 1) * width // 4)
            if kind == "in":
                ref[q] = row_in[:, at].astype(BF)
            else:
                cut = out[layer, :, at]
                ref[q] = jnp.concatenate([cut, jnp.zeros((8, width // 4), F32)], axis=0).astype(BF)


IN_SHAPES = [(4, PADDED[kind], width // 4) for kind, _, width, _ in PARTS]
OWN_SHAPES = [(BLOCK_ROWS[kind], width // 4) for kind, _, width, _ in PARTS]
GATHER_OUT = RESULT + KEPT + OPERANDS


def gather_kernel(*refs):
    refs = list(refs)
    take = lambda n: [refs.pop(0) for _ in range(n)]
    e48, e96 = take(2)
    matrices = take(4)
    conv, gain, head, tokens, lengths, owners = take(6)
    kept = dict(zip(MATRIX, take(2)))
    outs = dict(zip(MATRIX, take(2)))
    masks, lags, rows, heads = take(4)
    saved = take(len(GATHER_OUT))
    held = dict(zip(MATRIX, take(2)))
    temps = {entry[0]: refs.pop(0) for entry in GATHER_OUT + SMALL + STATES + WORK + LOW}
    (row_in,) = take(1)
    count = len(PARTS)
    ins = [take(count), take(count)]
    stages = [take(count), take(count)]
    owns = take(count)
    tiles, head_in, head_all, resid = take(4)
    send, recv, local = take(3)
    wire = Wire(send, recv)
    x, z, c, y = wire.x, wire.z, wire.core, wire.y
    device = (x * 8 + z * 2 + c) * 4 + y
    wire.greet()

    arrived = []
    def send_rows(layer):
        prepare_rows(matrices, layer, row_in, ins[layer])
        for n in range(count):
            stages[layer][n][y] = ins[layer][n][y]
            arrived.append(
                [
                    wire.copy(ins[layer][n].at[turn(y, by)], stages[layer][n].at[y], device_at(x, z, c, turn(y, by)))
                    for by in (1, 3, 2)
                ]
            )

    send_rows(0)
    send_rows(1)
    tiles[x, z, c, y] = small_tile(conv, gain, device)
    line = lax.broadcasted_iota(jnp.int32, (8, 128), 0)
    tile = jnp.zeros((8, 128), F32)
    for l in range(LAYERS):
        for j in range(3):
            part = jnp.pad(head[j, l : l + 1, :], ((0, 0), (0, 116)))
            tile = jnp.where(line == 3 * l + j, part, tile)
    tile = pltpu.roll(tile, 12 * y, 1)
    head_in[...] = tile
    head_all[y] = tile
    head_copies = [wire.copy(head_in, head_all.at[y], device_at(x, z, c, turn(y, by))) for by in (1, 3, 2)]

    def compact(layer, n):
        for made in arrived[count * layer + n]:
            made.wait_recv()
        got = stages[layer][n][...]
        flat = got.reshape(got.shape[0] * got.shape[1], got.shape[2])
        return dot((e96 if PARTS[n][0] == "out" else e48)[...], flat).astype(BF)

    for n, (kind, base, width, _) in enumerate(PARTS):
        held[kind][x, z, c, :, cols(base, y, width // 4)] = compact(0, n)

    plans = [
        [gather_regions(part, refs[part[0]], x, z, c, y) for part in PARTS] for refs in (held, outs)
    ]
    low = Gather(wire, plans[0] + [gather_regions(None, tiles, x, z, c, y)])
    top = Gather(wire, plans[1])
    top_in = Gather(wire, plans[1][: len(IN_PARTS)])
    low.start(0)
    placed = []
    for n, (kind, base, width, _) in enumerate(PARTS):
        owns[n][...] = compact(1, n)
        made = pltpu.make_async_copy(
            owns[n], outs[kind].at[x, z, c, :, cols(base, y, width // 4)], local.at[n]
        )
        made.start()
        placed.append(made)
    own_masks(lengths, owners, device, masks, lags)
    for made in head_copies:
        made.wait_recv()
    total = head_all[0] + head_all[1] + head_all[2] + head_all[3]
    for l in range(LAYERS):
        heads[l] = jnp.concatenate([total[3 * l : 3 * l + 3], jnp.zeros((5, 128), F32)], axis=0)
    resid[...] = tokens[...].astype(F32)
    for made in placed:
        made.wait()
    top.start(0)
    for phase in (0, 1):
        low.middle(phase)
        top.middle(phase)
        low.end(phase)
        low.start(phase + 1)
        top.end(phase)
        if phase == 0:
            top.start(1)
    low.middle(2)
    top_in.start(2)
    low.end(2)
    low.finish()
    stored = []
    for n, kind in enumerate(MATRIX):
        made = pltpu.make_async_copy(held[kind], kept[kind], local.at[count + n])
        made.start()
        stored.append(made)

    unpack_small(tiles, rows)
    m = Layer(0, resid=resid, mask=masks, lag=lags, rows=rows, heads=heads, **temps)
    forward(m, Held(held), mixed=lambda: top_in.middle(2))
    for n, entry in enumerate(GATHER_OUT):
        made = pltpu.make_async_copy(temps[entry[0]], saved[n], local.at[count + 2 + n])
        made.start()
        stored.append(made)
    top_in.end(2)
    top_in.finish()
    for made in stored:
        made.wait()
    wire.finish()


def gather_all(matrices, conv, gain, head, tokens, lengths, owners):
    copies = 2 * len(PARTS) * 3 + 3 + (2 * len(PARTS) + 1) * 18
    saved = GATHER_OUT
    temps = GATHER_OUT + SMALL + STATES + WORK + LOW
    out_shape = [jax.ShapeDtypeStruct(shape, BF) for shape in tuple(MATRIX.values()) * 2]
    out_shape += [
        jax.ShapeDtypeStruct(shape, F32)
        for shape in ((SLOTS, SLOTS), (SLOTS, SLOTS), ROWS_SHAPE, HEADS_SHAPE)
    ]
    out_shape += [jax.ShapeDtypeStruct(shape, kind) for _, shape, kind in saved]
    scratch = [pltpu.VMEM(shape, BF) for shape in MATRIX.values()]
    scratch += [pltpu.VMEM(shape, kind) for _, shape, kind in temps]
    scratch += [pltpu.VMEM((16, WIN), F32)]
    scratch += [pltpu.VMEM(shape, BF) for shape in IN_SHAPES * 4]
    scratch += [pltpu.VMEM(shape, BF) for shape in OWN_SHAPES]
    scratch += [
        pltpu.VMEM((4, 4, 2, 4, 16, 128), BF),
        pltpu.VMEM((8, 128), F32),
        pltpu.VMEM((4, 8, 128), F32),
        pltpu.VMEM((SLOTS, WIDTH), F32),
        pltpu.SemaphoreType.DMA((copies,)),
        pltpu.SemaphoreType.DMA((copies,)),
        pltpu.SemaphoreType.DMA((len(PARTS) + 2 + len(saved),)),
    ]
    made = pl.pallas_call(
        gather_kernel,
        out_shape=out_shape,
        in_specs=[VMEM] * 12,
        out_specs=[ANY] * 4 + [VMEM] * 4 + [ANY] * len(saved),
        scratch_shapes=scratch,
        compiler_params=pltpu.CompilerParams(
            collective_id=0, has_side_effects=True, vmem_limit_bytes=60 * 2**20
        ),
        name="gather_forward_first",
    )(
        jnp.asarray(picker(12, 16), BF),
        jnp.asarray(picker(24, 32), BF),
        *matrices, conv, gain, head, tokens, lengths, owners,
    )
    weights = [
        (w_in.reshape(WIDTH, WIN), w_out) for w_in, w_out in (made[:2], made[2:4])
    ]
    params = dict(zip(PARAMS, made[4:8]))
    return weights, params, {entry[0]: value for entry, value in zip(saved, made[8:])}


def adam(weight, moment, square, grad, rate, decay):
    moment = BETA_ONE * moment + (1.0 - BETA_ONE) * grad
    square = BETA_TWO * square + (1.0 - BETA_TWO) * grad * grad
    corr_one = 1.0 - BETA_ONE**STEP
    corr_two = 1.0 - BETA_TWO**STEP
    weight = weight - rate * (
        moment / corr_one / (jnp.sqrt(square / corr_two) + ADAM_EPS) + decay * weight
    )
    return (weight, moment, square)


RATES = ((RATE_MATRIX, WEIGHT_DECAY),) * 4 + ((RATE_VECTOR, 0.0),) * 2 + ((RATE_HEADS, 0.0),)


def update_kernel(count, *refs):
    refs = list(refs)
    take = lambda n: [refs.pop(0) for _ in range(n)]
    hbm, results, held = take(count), take(28), take(count)
    (arrive,) = take(1)
    fetched = [pltpu.make_async_copy(src, dst, arrive.at[n]) for n, (src, dst) in enumerate(zip(hbm, held))]
    for made in fetched:
        made.start()
    for made in fetched:
        made.wait()
    refs = held + results
    summed = [take(len(PARTS) + 1) for _ in range(LAYERS)]
    olds = [take(3) for _ in range(7)]
    news = [take(3) for _ in range(7)]
    inner, state, step, out, conv, gain, head = take(7)
    places = ((inner, 0, INNER, 0), (state, INNER, CONVED, 0), (step, DT_AT, DT_AT + HEADS, 0), (inner, WA, WIN, INNER))
    x, z, c, y = place()
    device = (x * 8 + z * 2 + c) * 4 + y
    for layer, (*sums, tile) in enumerate(summed):
        at = slice(layer, layer + 1)
        for (kind, base, width, _), cut in zip(PARTS, sums):
            size = width // 4
            for q in range(4):
                part = cut[q].astype(F32)
                start = base + q * size
                if kind == "out":
                    out[layer, :, start : start + size] = part[:24]
                    continue
                for ref, low, high, to in places:
                    first, last = max(low, start), min(high, start + size)
                    if first < last:
                        for r in range(12):
                            ref[r, at, to + first - low : to + last - low] = part[
                                r : r + 1, first - start : last - start
                            ]
        taps = pltpu.roll(tile[...], lax.rem(SLOTS * 32 - 26 * device, 128), 1)
        norms = pltpu.roll(tile[...], lax.rem(SLOTS * 64 - 36 * device, 128), 1)
        mine = pltpu.roll(tile[...], lax.rem(SLOTS - 12 * y, 128), 1)
        for k in range(5):
            conv[k, at, :] = taps[k : k + 1, :26]
        gain[at, :] = norms[5:6, :36]
        head[0, at, :] = mine[6:7, :12]
        head[1, at, :] = mine[7:8, :12]
        head[2, at, :] = mine[6:7, 64:76]

    for old, new, grad, (rate, decay) in zip(olds, news, (inner, state, step, out, conv, gain, head), RATES):

        def body(at, old=old, new=new, grad=grad, rate=rate, decay=decay):
            values = adam(old[0][at], old[1][at], old[2][at], grad[at], rate, decay)
            for ref, value in zip(new, values):
                ref[at] = value

        if grad.shape[0] == 12:

            @pl.loop(0, 12)
            def _(r, body=body):
                body(r)
        else:
            body(...)


def update_all(summed, olds):
    flat = [ref for item in summed for ref in item] + [ref for item in olds for ref in item]
    shapes = [jax.ShapeDtypeStruct(item[0].shape, F32) for item in olds]
    return pl.pallas_call(
        partial(update_kernel, len(flat)),
        out_shape=[shape for shape in shapes for _ in range(3)] + shapes,
        in_specs=[ANY] * len(flat),
        out_specs=[VMEM] * 28,
        scratch_shapes=[pltpu.VMEM(item.shape, item.dtype) for item in flat]
        + [pltpu.SemaphoreType.DMA((len(flat),))],
        compiler_params=pltpu.CompilerParams(vmem_limit_bytes=62 * 2**20),
        name="update",
    )(*flat)


def shards(
    tokens,
    cotangent,
    seq_lengths,
    seq_owner,
    inner_weight,
    inner_moment,
    inner_square,
    state_weight,
    state_moment,
    state_square,
    step_weight,
    step_moment,
    step_square,
    out_weight,
    out_moment,
    out_square,
    conv_weight,
    conv_moment,
    conv_square,
    gains,
    gain_moment,
    gain_square,
    head_params,
    head_moment,
    head_square,
):
    middle = lambda v: v.transpose(1, 0, 2)
    last = lambda v: v.transpose(2, 0, 1)
    same = lambda v: v
    views = (
        (middle, middle, (inner_weight, inner_moment, inner_square)),
        (middle, middle, (state_weight, state_moment, state_square)),
        (middle, middle, (step_weight, step_moment, step_square)),
        (same, same, (out_weight, out_moment, out_square)),
        (last, lambda v: v.transpose(1, 2, 0), (conv_weight, conv_moment, conv_square)),
        (same, same, (gains, gain_moment, gain_square)),
        (middle, middle, (head_params, head_moment, head_square)),
    )
    olds = [[view(item) for item in items] for view, _, items in views]
    firsts = [item[0] for item in olds]
    weights, params, low = gather_all(
        firsts[:4], firsts[4], firsts[5], firsts[6], tokens, seq_lengths.reshape(1, 256), seq_owner.reshape(1, 256)
    )
    top = last_layer(weights[1], params, [("resid", low["resid_out"]), ("upstream", cotangent)])
    below = [("resid", tokens), ("upstream", top["upstream_out"])] + [(key, low[key]) for key, _, _ in KEPT]
    sums_top, bottom = reduce_layer("reduce_last_backward_first", 1, top, weights[0], params, below)
    sums_low, _ = reduce_layer("reduce_first", 2, {**low, **bottom})
    made = update_all([sums_low, sums_top], olds)
    results = [top["resid_out"], bottom["upstream_out"]]
    for n, (_, back, _) in enumerate(views):
        results += [back(item) for item in made[3 * n : 3 * n + 3]]
    results += [back(item) for (_, back, _), item in zip(views, made[21:])]
    return tuple(results)


ROWS = P(("fsdp", "sub"), None)
SPLIT = P(None, ("fsdp", "sub"), None)
FLAT = P(None, ("fsdp", "sub"))
HEAD = P(None, None, "sub")


def solution(mesh):
    return jax.shard_map(
        shards,
        mesh=mesh,
        in_specs=(ROWS, ROWS, P(), P()) + (SPLIT,) * 15 + (FLAT,) * 3 + (HEAD,) * 3,
        out_specs=(ROWS, ROWS) + (SPLIT,) * 15 + (FLAT,) * 3 + (HEAD,) * 3 + (SPLIT,) * 5 + (FLAT, HEAD),
        check_vma=False,
    )
```

time: 2490 us -> 380 us (0.15)
  waiting for transfers between devices: 1090 us -> 0 us
  blocking collectives: 542 us -> 0 us
  local copies, waits for them, and re-layouts: 540 us -> 1.77 us
  Pallas kernels: 0 us -> 378 us
  matrix products: 221 us -> 0 us
  other arithmetic: 69.7 us -> 0 us
    reduce_scatter x2 -> x0, waiting for transfers between devices: 1080 us -> none  [reduce_grads(): lax.psum_scatter(joined, ('fsdp', 'sub'), scatter_dimension=0, tiled=True)]
    all_gather x7 -> x0, blocking collectives: 403 us -> none  [the longest x2 137 us: fetch(): lax.all_gather(mat_bc, ('fsdp', 'sub'), axis=0, tiled=True)]
    pallas_call x0 -> x5, Pallas kernels: none -> 378 us  [the longest x2 177 us: reduce_layer(): pl.pallas_call(kernel, out_shape=out_shape, in_specs=[VMEM] * 2 + [ANY] *...]
    dot_general x36 -> x0, matrix products: 221 us -> none  [the longest x2 51.2 us: layer_backward(): jnp.einsum('tk,dk->td', d_zx, mat_zx, preferred_element_type=jnp.float32)]
    reshape x20 -> x0, local copies, waits for them, and re-layouts: 220 us -> none  [the longest x12 122 us: reduce_grads(): flat_rows = [grad.reshape(devices, -1) for grad in grads]]
    unnamed x409 -> x6, local copies, waits for them, and re-layouts: 206 us -> 1.77 us
    pad x2 -> x0, local copies, waits for them, and re-layouts: 78.4 us -> none  [reduce_grads(): jnp.pad(joined, ((0, 0), (0, padded - length_all)))]
    psum x1 -> x0, blocking collectives: 70.8 us -> none  [shards(): head_total = lax.psum(jnp.stack(head_terms), ('fsdp', 'sub'))]
  transfers between devices with their start and end apart: 6 -> 0, of which waited for: 2 -> 0; matrix products, arithmetic and copies ran while one was open for 17% -> 0% of each run, Pallas kernels for 0% -> 0%
where the time goes in v1:
time: 380 us
  Pallas kernels  378 us (99%)
    pallas_call x2, Pallas kernels, reduce_layer(): pl.pallas_call(kernel, out_shape=out_shape, in_specs=[VMEM] * 2 + [ANY] *...  177 us
    pallas_call x1, Pallas kernels, gather_all(): pl.pallas_call(gather_kernel, out_shape=out_shape, in_specs=[VMEM] * 12,...  133 us
    pallas_call x1, Pallas kernels, last_layer(): pl.pallas_call(kernel, out_shape=[jax.ShapeDtypeStruct(shape, kind) for _...  61.7 us

profile of v1, /device:TPU:0, one launch (start us, length us, event | category | flops | bytes accessed | tf_op | source)
XLA Modules:
  0.0 380.2 jit_solution(14151944167122626274)
XLA Ops:
  0.7 133.1 %gather_forward_first.1 = (bf16[4,4,2,48,6656]{4,3,2,1,0:T(8,128)(2,1)}, bf16[4,4,2,96,1536]{4,3,2,1,0:T(8,128)(2,1)}, bf16[4,4,2,48,6656]{4,3,2,1,0:T(8,128)(2,...) custom-call(bf16[48,64]{1,0:T(8,128)(2,1)} %constant.8.clone.refs_0_, ...), custom_call_target="tpu_custom_call" | custom-call | tf_op jit(solution)/shard_map/gather_forward_first/pallas_call | solution.py:1371
  133.8 61.7 %forward_backward_last.1 = (f32[128,1536]{1,0:T(8,128)}, bf16[1536,128]{1,0:T(8,128)(2,1)}, bf16[3072,128]{1,0:T(8,128)(2,1)}, f32[128,1536]{1,0:T(8,128)}, bf16...) custom-call(bf16[1536,6656]{1,0:T(8,128)(2,1)} %bitcast.44, ...), custom_call_target="tpu_custom_call" | custom-call | tf_op jit(solution)/shard_map/forward_backward_last/pallas_call | solution.py:1007
  195.5 92.6 %reduce_last_backward_first.1 = (bf16[4,16,640]{2,1,0:T(8,128)(2,1)}, bf16[4,16,512]{2,1,0:T(8,128)(2,1)}, bf16[4,16,512]{2,1,0:T(8,128)(2,1)}, bf16[4,32,128]{2...) custom-call(bf16[64,48]{1,0:T(8,128)(2,1)} %constant.10.clone.refs_0, ...), custom_call_target="tpu_custom_call" | custom-call | tf_op jit(solution)/shard_map/reduce_last_backward_first/pallas_call | solution.py:1114
  288.1 84.2 %reduce_first.1 = (bf16[4,16,640]{2,1,0:T(8,128)(2,1)}, bf16[4,16,512]{2,1,0:T(8,128)(2,1)}, bf16[4,16,512]{2,1,0:T(8,128)(2,1)}, bf16[4,32,128]{2,1,0:T(8,128)(...) custom-call(bf16[64,48]{1,0:T(8,128)(2,1)} %constant.10.clone.refs_0_, ...), custom_call_target="tpu_custom_call" | custom-call | tf_op jit(solution)/shard_map/reduce_first/pallas_call | solution.py:1114
  372.3 0.0 copy-start
  372.4 0.0 copy-start.1
  372.4 6.0 %update.1 = (f32[12,2,6144]{2,1,0:T(2,128)}, f32[12,2,6144]{2,1,0:T(2,128)}, f32[12,2,6144]{2,1,0:T(2,128)}, f32[12,2,256]{2,1,0:T(2,128)}, f32[12,2,256]{2,1,0:...) custom-call(bf16[4,16,640]{2,1,0:T(8,128)(2,1)} %get-tuple-element.1, ...), custom_call_target="tpu_custom_call" | custom-call | tf_op jit(solution)/shard_map/update/pallas_call | solution.py:1471
  378.4 0.0 copy-done
  378.4 0.9 copy.63
  379.3 0.0 copy-done.1
  379.3 0.9 copy.64
Async XLA Ops:
  372.3 6.0 %copy-start = (f32[128,1536]{1,0:T(8,128)S(1)}, f32[128,1536]{1,0:T(8,128)}, u32[]{:S(2)}) copy-start(f32[128,1536]{1,0:T(8,128)} %get-tuple-element.198) | copy-start | bytes 2359300
  372.4 6.9 %copy-start.1 = (f32[128,1536]{1,0:T(8,128)S(1)}, f32[128,1536]{1,0:T(8,128)}, u32[]{:S(2)}) copy-start(f32[128,1536]{1,0:T(8,128)} %get-tuple-element.199) | copy-start | bytes 2359300
